TPU v7x, 32 devices: a whole 2x2x4 slice. The times are simulated.
32 devices in a mesh: ens: 4 (over z), lon: 2 (over y), lat: 4 (over x, core).
Axes of the slice: x: 2, y: 2, z: 4, core: 2. Of those that a mesh axis runs over, the one named last changes fastest.
Arguments:
- ocean_state: bfloat16 [4, 200, 32, 256], P('ens', None, 'lat', 'lon'), may hold values from -6 to 6
- ocean_mask: int32 [32, 256], P('lat', 'lon'), may hold values from 0 to 1, as said below
- dw_weight: float32 [200, 49], replicated, may hold values from -0.875 to 0.875
- norm_gain: float32 [200], replicated, may hold values from 0.1 to 1.9
- expand_weight: bfloat16 [200, 800], replicated, may hold values from -0.4375 to 0.4375
- reduce_weight: bfloat16 [800, 200], replicated, may hold values from -0.21875 to 0.21875
- cotangent: bfloat16 [4, 200, 32, 256], P('ens', None, 'lat', 'lon'), may hold values from -6 to 6
Outputs:
- next_state: bfloat16 [4, 200, 32, 256], P('ens', None, 'lat', 'lon')
- grad_depthwise: float32 [200, 49], replicated
- grad_gain: float32 [200], replicated
- grad_expand: float32 [200, 800], replicated
- grad_reduce: float32 [800, 200], replicated
Inputs may be any that keep to these rules, and one draw needn't show every extreme that they name: `ocean_mask`: the share of ocean cells differs from tile to tile of 8 x 128 cells, from about a third to nearly all.
All inputs are finite; a program needn't handle non-finite values.
Results may differ from a plain program's by a relative error of at most 0.0058.
Values may be sent and summed in bfloat16 or wider, within the bound.
A program may use at most 64 MiB of HBM per device.

v0:
```python
import math

import jax
import jax.numpy as jnp
from jax import lax
from jax.sharding import PartitionSpec as P

KS = 7


norm_eps = 1e-06
root_half = 0.7071067811865476
gauss_norm = 0.3989422804014327


def with_halo(cells, sides, width):
    for axis, dim in sides:
        count = lax.axis_size(axis)
        head = lax.slice_in_dim(cells, 0, width, axis=dim)
        tail = lax.slice_in_dim(cells, cells.shape[dim] - width, cells.shape[dim], axis=dim)
        cells = jnp.concatenate(
            [
                lax.ppermute(tail, axis, [(i, (i + 1) % count) for i in range(count)]),
                cells,
                lax.ppermute(head, axis, [((i + 1) % count, i) for i in range(count)]),
            ],
            axis=dim,
        )
    return cells


def swapped(array, axis, stride):
    return lax.ppermute(array, axis, [(i, i ^ 1 << stride) for i in range(lax.axis_size(axis))])


def depthwise(padded, dw_weight, out_rows, out_cols):
    conv_sum = jnp.zeros((padded.shape[0], out_rows, out_cols), jnp.float32)
    for shift_a in range(KS):
        for shift_b in range(KS):
            tap_weight = dw_weight[:, shift_a * KS + shift_b][:, None, None]
            window = padded[:, shift_a : shift_a + out_rows, shift_b : shift_b + out_cols].astype(
                jnp.float32
            )
            conv_sum = conv_sum + tap_weight * window
    return conv_sum


def depthwise_grad(d_conv, padded, out_rows, out_cols):
    columns = []
    for shift_a in range(KS):
        for shift_b in range(KS):
            window = padded[:, shift_a : shift_a + out_rows, shift_b : shift_b + out_cols].astype(
                jnp.float32
            )
            columns.append(jnp.sum(d_conv * window, axis=(1, 2)))
    return jnp.stack(columns, axis=1)


def cell_pass(conv_blk, state_blk, cot_blk, mask_blk, norm_gain, expand_weight, reduce_weight):
    chan_mean = jnp.mean(conv_blk, axis=0, keepdims=True)
    centred = conv_blk - chan_mean
    chan_var = jnp.mean(centred * centred, axis=0, keepdims=True)
    inv_std = lax.rsqrt(chan_var + norm_eps)
    normed = centred * inv_std
    scaled = (normed * norm_gain[:, None]).astype(jnp.bfloat16)
    pre_act = jnp.dot(expand_weight.T, scaled, preferred_element_type=jnp.float32)
    normal_cdf = 0.5 * (1.0 + lax.erf(pre_act * root_half))
    normal_pdf = jnp.exp(-0.5 * pre_act * pre_act) * gauss_norm
    hidden = (pre_act * normal_cdf).astype(jnp.bfloat16)
    gelu_slope = normal_cdf + pre_act * normal_pdf
    branch = jnp.dot(reduce_weight.T, hidden, preferred_element_type=jnp.float32)
    out_blk = ((state_blk.astype(jnp.float32) + branch) * mask_blk[None, :]).astype(jnp.bfloat16)
    grad_reduce = jnp.dot(hidden, cot_blk.T, preferred_element_type=jnp.float32)
    d_hidden = jnp.dot(reduce_weight, cot_blk, preferred_element_type=jnp.float32)
    d_pre = (d_hidden * gelu_slope).astype(jnp.bfloat16)
    grad_expand = jnp.dot(scaled, d_pre.T, preferred_element_type=jnp.float32)
    d_scaled = jnp.dot(expand_weight, d_pre, preferred_element_type=jnp.float32)
    grad_gain = jnp.sum(d_scaled * normed, axis=1)
    d_normed = d_scaled * norm_gain[:, None]
    d_conv = inv_std * (
        d_normed
        - jnp.mean(d_normed, axis=0, keepdims=True)
        - normed * jnp.mean(d_normed * normed, axis=0, keepdims=True)
    )
    return (out_blk, d_conv, grad_expand, grad_reduce, grad_gain)


def body(ocean_state, ocean_mask, dw_weight, norm_gain, expand_weight, reduce_weight, cotangent):
    state_tile = ocean_state[0]
    channels = state_tile.shape[0]
    tile_rows = state_tile.shape[1]
    tile_cols = state_tile.shape[2]
    margin = KS // 2
    mask_bf = ocean_mask.astype(jnp.bfloat16)
    masked = state_tile * mask_bf[None]
    padded = with_halo(masked, (("lon", 2), ("lat", 1)), margin)
    lat_now = lax.axis_index("lat")
    lat_count = lax.axis_size("lat")
    lon_count = lax.axis_size("lon")
    top_strip = padded[:, tile_rows : tile_rows + margin, :][:, ::-1, ::-1]
    mirrored = top_strip
    for bit_number in range(lon_count.bit_length() - 1):
        mirrored = swapped(mirrored, "lon", bit_number)
    north_rows = jnp.where(lat_now == lat_count - 1, mirrored, padded[:, tile_rows + margin :, :])
    south_rows = jnp.where(lat_now == 0, jnp.zeros_like(top_strip), padded[:, :margin, :])
    padded = jnp.concatenate(
        [south_rows, padded[:, margin : tile_rows + margin, :], north_rows], axis=1
    )
    conv_out = depthwise(padded, dw_weight, tile_rows, tile_cols)
    cell_count = tile_rows * tile_cols
    cot_masked = (cotangent[0] * mask_bf[None]).reshape(channels, cell_count)
    out_flat, d_conv, grad_expand, grad_reduce, grad_gain = cell_pass(
        conv_out.reshape(channels, cell_count),
        state_tile.reshape(channels, cell_count),
        cot_masked,
        ocean_mask.astype(jnp.float32).reshape(cell_count),
        norm_gain,
        expand_weight,
        reduce_weight,
    )
    grad_depthwise = depthwise_grad(
        d_conv.reshape(channels, tile_rows, tile_cols), padded, tile_rows, tile_cols
    )
    grad_scale = 1.0 / math.sqrt(lax.axis_size("ens") * lat_count * lon_count * cell_count)
    grad_expand = grad_expand * grad_scale
    grad_reduce = grad_reduce * grad_scale
    grad_gain = grad_gain * grad_scale
    grad_depthwise = grad_depthwise * grad_scale
    grad_expand, grad_reduce, grad_gain, grad_depthwise = lax.psum(
        (grad_expand, grad_reduce, grad_gain, grad_depthwise), ("ens", "lon", "lat")
    )
    next_state = out_flat.reshape(channels, tile_rows, tile_cols)[None]
    return (next_state, grad_depthwise, grad_gain, grad_expand, grad_reduce)


def solution(mesh):
    return jax.shard_map(
        body,
        mesh=mesh,
        in_specs=(
            P("ens", None, "lat", "lon"),
            P("lat", "lon"),
            P(),
            P(),
            P(),
            P(),
            P("ens", None, "lat", "lon"),
        ),
        out_specs=(P("ens", None, "lat", "lon"), P(), P(), P(), P()),
        check_vma=False,
    )
```

profile of v0, /device:TPU:0, one launch (start us, length us, event | category | flops | bytes accessed | tf_op | source)
XLA Modules:
  0.0 198.5 jit_solution(6079324291934809230)
XLA Ops:
  7.2 1.4 convert_bitcast_fusion
  8.6 1.3 copy.12
  10.1 3.0 %collective-permute-start = (bf16[200,8,3]{0,2,1:T(4,128)(2,1)S(1)}, bf16[200,8,3]{0,2,1:T(4,128)(2,1)S(1)}, u32[]{:S(2)}, u32[]{:S(2)}) collective-permute-start(bf16[200,8,3]{0,2,1:T(4,128)(2,1)S(1)} %get-tuple-element.80), channel_id=1, source_target_pairs={{0,4},{4,0},{1,5},{5,1},{2,6},{6,2},{3,7},{7,3},{8,12},{12,8},{9,1... | collective-permute-start | bytes 28808 | tf_op jit(solution)/shard_map/ppermute | solution.py:23
  13.2 1.6 collective-permute-done
  14.8 2.0 %collective-permute-done.1 = bf16[200,8,3]{0,2,1:T(4,128)(2,1)S(1)} collective-permute-done((bf16[200,8,3]{0,2,1:T(4,128)(2,1)S(1)}, bf16[200,8,3]{0,2,1:T(4,128)(2,1)S(1)}, u32[]{:S(2)}, u32[]{:S(2)}) %collective-permute-start.1) | collective-permute-done | bytes 9632 | tf_op jit(solution)/shard_map/ppermute | solution.py:25
  18.3 1.6 collective-permute-start.4
  19.9 2.3 %collective-permute-done.2 = bf16[200,3,134]{0,2,1:T(8,128)(2,1)S(1)} collective-permute-done((bf16[200,3,134]{0,2,1:T(8,128)(2,1)S(1)}, bf16[200,3,134]{0,2,1:T(8,128)(2,1)S(1)}, u32[]{:S(2)}, u32[]{:S(2)}) %collective-permute-start.2) | collective-permute-done | bytes 160832 | tf_op jit(solution)/shard_map/ppermute | solution.py:23
  22.3 3.3 %collective-permute-done.3 = bf16[200,3,134]{0,2,1:T(8,128)(2,1)S(1)} collective-permute-done((bf16[200,3,134]{0,2,1:T(8,128)(2,1)S(1)}, bf16[200,3,134]{0,2,1:T(8,128)(2,1)S(1)}, u32[]{:S(2)}, u32[]{:S(2)}) %collective-permute-start.3) | collective-permute-done | bytes 160832 | tf_op jit(solution)/shard_map/ppermute | solution.py:33
  25.9 8.3 %fusion.118 = (f32[8,128]{1,0:T(8,128)S(1)}, f32[200,8,128]{0,2,1:T(8,128)S(1)}) fusion(bf16[200,11,134]{0,2,1:T(8,128)(2,1)S(1)} %get-tuple-element.77, f32[200]{0:T(256)S(1)} %bitcast.303, f32[200]{0:T(256)S(1)} %bitcast.304, f32[200]{0:T(256)S(1)} %bitcast.257, f32[200]{0:T(256)S(1)} %bitcast.258, f32[200]{0:T(256)S(1)} %bitcast.259, ...), kind=kLoop, calls=%fused_computation.252 | loop fusion | flops 33790976 | bytes 18494496 | tf_op jit(solution)/shard_map/reduce_sum | solution.py:60
  35.2 1.5 copy.62
  36.8 2.2 %fusion.9 = (bf16[800,1024]{1,0:T(8,128)(2,1)}, f32[1024,800]{0,1:T(8,128)S(1)}) fusion(bf16[200,800]{1,0:T(8,128)(2,1)S(1)} %copy-done, f32[200,1024]{1,0:T(8,128)S(1)} %copy.62, f32[200]{0:T(256)S(1)} %copy-done.8, f32[1024]{0:T(1024)S(1)} %rsqrt_bitcast_fusion, f32[1024]{0:T(1024)S(1)} %get-tuple-element.133), kind=kOutput, calls=%fused_computation.12 | convolution fusion | flops 332595200 | bytes 6063392 | tf_op jit(solution)/shard_map/dot_general | solution.py:66
  39.0 1.7 fusion.5
  40.7 1.7 convolution_multiply_fusion.1
  42.4 1.4 multiply_reduce_fusion.1
  43.7 1.3 multiply_reduce_fusion.2
  45.0 1.5 copy.63
  46.5 3.8 %fusion.59 = (f32[200]{0:T(256)S(1)}, f32[200]{0:T(256)S(1)}, f32[200]{0:T(256)S(1)}, f32[200]{0:T(256)S(1)}, f32[200]{0:T(256)S(1)}, /*index=5*/f32[200]{0:T(25...) fusion(bf16[200,11,134]{0,2,1:T(8,128)(2,1)S(1)} %get-tuple-ele, ...), kind=kLoop, calls=%fused_computation.162 | loop fusion | flops 11055600 | bytes 8206400 | tf_op jit(solution)/shard_map/reduce_sum | solution.py:55
  50.3 3.8 %fusion.109 = (f32[200]{0:T(256)}, f32[200]{0:T(256)}, f32[200]{0:T(256)}, f32[200]{0:T(256)}, f32[200]{0:T(256)}, /*index=5*/f32[200]{0:T(256)}, f32[200]{0:T(2...) fusion(bf16[200,11,134]{0,2,1:T(8,128)(2,1)S(1)} %get-tuple-ele, ...), kind=kLoop, calls=%fused_computation.212 | loop fusion | flops 11055600 | bytes 8206400 | tf_op jit(solution)/shard_map/reduce_sum | solution.py:55
  54.0 1.6 convolution_multiply_fusion
  55.7 3.0 %fusion.91 = (f32[200]{0:T(256)}, f32[200]{0:T(256)}, f32[200]{0:T(256)}, f32[200]{0:T(256)}, f32[200]{0:T(256)}, /*index=5*/f32[200]{0:T(256)}, f32[200]{0:T(25...) fusion(bf16[200,11,134]{0,2,1:T(8,128)(2,1)S(1)} %get-tuple-element.77, ...), kind=kLoop, calls=%fused_computation.194 | loop fusion | flops 11056800 | bytes 3715200 | tf_op jit(solution)/shard_map/reduce_sum | solution.py:55
  59.1 1.6 fusion.13
  62.1 41.1 %all-reduce = (f32[200,49]{0,1:T(8,128)}, f32[200]{0:T(256)}) all-reduce(f32[200,49]{0,1:T(8,128)S(1)} %broadcast_multiply_fusion, f32[200]{0:T(256)S(1)} %broadcast_multiply_fusion.4), channel_id=1, replica_groups=mesh['ens'=4,'lon'=2,'lat'=4] {'ens','lon','lat'}, use_global_device_ids=true, to_apply=%region_53.54 | all-reduce | flops 10000 | bytes 80000 | tf_op jit(solution)/shard_map/psum | solution.py:129
  103.2 85.5 %all-reduce.4.cloned.1.call-done = (f32[200,800]{1,0:T(8,128)}, f32[800,200]{0,1:T(8,128)}) async-done(((f32[200,800]{1,0:T(8,128)}, f32[800,200]{0,1:T(8,128)}), (f32[200,800]{1,0:T(8,128)}, f32[800,200]{0,1:T(8,128)})) %all-reduce.4.cloned.1.call-update) | async-done | bytes 1280016 | tf_op jit(solution)/shard_map/psum | solution.py:129
  188.7 2.1 %copy.74 = f32[200,800]{1,0:T(8,128)} copy(f32[200,800]{1,0:T(8,128)} %get-tuple-element.143) | data formatting | bytes 1280000
  (125 shorter events, 5.1 us)
Async XLA Ops:
  7.2 29.6 %copy-start = (bf16[200,800]{1,0:T(8,128)(2,1)S(1)}, bf16[200,800]{1,0:T(8,128)(2,1)}, u32[]{:S(2)}) copy-start(bf16[200,800]{1,0:T(8,128)(2,1)} %param.11) | copy-start | bytes 960004
  7.2 6.0 %copy-start.7 = (f32[200,49]{0,1:T(8,128)S(1)}, f32[200,49]{0,1:T(8,128)}, u32[]{:S(2)}) copy-start(f32[200,49]{0,1:T(8,128)} %param.9) | copy-start | bytes 117604
  7.2 181.5 %all-reduce.4.cloned.1.call-start = ((), (), s32[]{:S(2)}) async-start(), calls=%async_computation | async-start | bytes 2867200 | tf_op jit(solution)/shard_map/psum | solution.py:129
  10.1 4.8 %collective-permute-start = (bf16[200,8,3]{0,2,1:T(4,128)(2,1)S(1)}, bf16[200,8,3]{0,2,1:T(4,128)(2,1)S(1)}, u32[]{:S(2)}, u32[]{:S(2)}) collective-permute-start(bf16[200,8,3]{0,2,1:T(4,128)(2,1)S(1)} %get-tuple-element.80), channel_id=1, source_target_pairs={{0,4},{4,0},{1,5},{5,1},{2,6},{6,2},{3,7},{7,3},{8,12},{12,8},{9,1... | collective-permute-start | bytes 28808 | tf_op jit(solution)/shard_map/ppermute | solution.py:23
  13.1 3.7 %collective-permute-start.1 = (bf16[200,8,3]{0,2,1:T(4,128)(2,1)S(1)}, bf16[200,8,3]{0,2,1:T(4,128)(2,1)S(1)}, u32[]{:S(2)}, u32[]{:S(2)}) collective-permute-start(bf16[200,8,3]{0,2,1:T(4,128)(2,1)S(1)} %get-tuple-element.81), channel_id=1, source_target_pairs={{4,0},{0,4},{5,1},{1,5},{6,2},{2,6},{7,3},{3,7},{12,8},{8,12},{13,... | collective-permute-start | bytes 28808 | tf_op jit(solution)/shard_map/ppermute | solution.py:25
  17.0 5.3 %collective-permute-start.2 = (bf16[200,3,134]{0,2,1:T(8,128)(2,1)S(1)}, bf16[200,3,134]{0,2,1:T(8,128)(2,1)S(1)}, u32[]{:S(2)}, u32[]{:S(2)}) collective-permute-start(bf16[200,3,134]{0,2,1:T(8,128)(2,1)S(1)} %get-tuple-element.79), channel_id=1, source_target_pairs={{0,1},{1,2},{2,3},{3,0},{4,5},{5,6},{6,7},{7,4},{8,9},{9,10},{10,1... | collective-permute-start | bytes 482408 | tf_op jit(solution)/shard_map/ppermute | solution.py:23
  18.1 7.5 %collective-permute-start.3 = (bf16[200,3,134]{0,2,1:T(8,128)(2,1)S(1)}, bf16[200,3,134]{0,2,1:T(8,128)(2,1)S(1)}, u32[]{:S(2)}, u32[]{:S(2)}) collective-permute-start(bf16[200,3,134]{0,2,1:T(8,128)(2,1)S(1)} %rev.3), channel_id=1, source_target_pairs={{0,4},{4,0},{1,5},{5,1},{2,6},{6,2},{3,7},{7,3},{8,12},{12,8},{9,1... | collective-permute-start | bytes 482408 | tf_op jit(solution)/shard_map/ppermute | solution.py:33
  18.3 7.3 %collective-permute-start.4 = (bf16[200,3,134]{0,2,1:T(8,128)(2,1)S(1)}, bf16[200,3,134]{0,2,1:T(8,128)(2,1)S(1)}, u32[]{:S(2)}, u32[]{:S(2)}) collective-permute-start(bf16[200,3,134]{0,2,1:T(8,128)(2,1)S(1)} %get-tuple-element.78), channel_id=1, source_target_pairs={{1,0},{2,1},{3,2},{0,3},{5,4},{6,5},{7,6},{4,7},{9,8},{10,9},{11,1... | collective-permute-start | bytes 482408 | tf_op jit(solution)/shard_map/ppermute | solution.py:25
  50.2 3.8 %copy-start.2 = (bf16[800,1024]{1,0:T(8,128)(2,1)S(1)}, bf16[800,1024]{1,0:T(8,128)(2,1)}, u32[]{:S(2)}) copy-start(bf16[800,1024]{1,0:T(8,128)(2,1)} %get-tuple-element.135) | copy-start | bytes 4915204
  50.3 3.8 %copy-start.48 = (bf16[1,200,8,128]{3,2,1,0:T(8,128)(2,1)S(1)}, bf16[1,200,8,128]{3,2,1,0:T(8,128)(2,1)}, u32[]{:S(2)}) copy-start(bf16[1,200,8,128]{3,2,1,0:T(8,128)(2,1)} %param.13) | copy-start | bytes 1228804
  55.7 3.1 %copy-start.3 = (bf16[800,1024]{1,0:T(8,128)(2,1)S(1)}, bf16[800,1024]{1,0:T(8,128)(2,1)}, u32[]{:S(2)}) copy-start(bf16[800,1024]{1,0:T(8,128)(2,1)} %get-tuple-element.135) | copy-start | bytes 4915204
  55.7 3.1 %copy-start.5 = (bf16[1,200,8,128]{3,2,1,0:T(8,128)(2,1)S(1)}, bf16[1,200,8,128]{3,2,1,0:T(8,128)(2,1)}, u32[]{:S(2)}) copy-start(bf16[1,200,8,128]{3,2,1,0:T(8,128)(2,1)} %param.7) | copy-start | bytes 1228804
  55.7 3.1 %copy-start.33 = (f32[1024]{0:T(1024)S(1)}, f32[1024]{0:T(1024)}, u32[]{:S(2)}) copy-start(f32[1024]{0:T(1024)} %get-tuple-element.131) | copy-start | bytes 12292
  58.8 2.8 %copy-start.9 = (f32[200]{0:T(256)S(1)}, f32[200]{0:T(256)}, u32[]{:S(2)}) copy-start(f32[200]{0:T(256)} %get-tuple-element.38) | copy-start | bytes 2404
  58.8 2.8 %copy-start.10 = (f32[200]{0:T(256)S(1)}, f32[200]{0:T(256)}, u32[]{:S(2)}) copy-start(f32[200]{0:T(256)} %get-tuple-element.39) | copy-start | bytes 2404
  58.8 2.8 %copy-start.11 = (f32[200]{0:T(256)S(1)}, f32[200]{0:T(256)}, u32[]{:S(2)}) copy-start(f32[200]{0:T(256)} %get-tuple-element.40) | copy-start | bytes 2404
  58.8 2.8 %copy-start.12 = (f32[200]{0:T(256)S(1)}, f32[200]{0:T(256)}, u32[]{:S(2)}) copy-start(f32[200]{0:T(256)} %get-tuple-element.41) | copy-start | bytes 2404
  58.8 2.8 %copy-start.13 = (f32[200]{0:T(256)S(1)}, f32[200]{0:T(256)}, u32[]{:S(2)}) copy-start(f32[200]{0:T(256)} %get-tuple-element.42) | copy-start | bytes 2404
  58.8 2.8 %copy-start.14 = (f32[200]{0:T(256)S(1)}, f32[200]{0:T(256)}, u32[]{:S(2)}) copy-start(f32[200]{0:T(256)} %get-tuple-element.43) | copy-start | bytes 2404
  58.8 2.8 %copy-start.15 = (f32[200]{0:T(256)S(1)}, f32[200]{0:T(256)}, u32[]{:S(2)}) copy-start(f32[200]{0:T(256)} %get-tuple-element.5) | copy-start | bytes 2404
  58.8 2.8 %copy-start.16 = (f32[200]{0:T(256)S(1)}, f32[200]{0:T(256)}, u32[]{:S(2)}) copy-start(f32[200]{0:T(256)} %get-tuple-element.6) | copy-start | bytes 2404
  58.9 2.8 %copy-start.17 = (f32[200]{0:T(256)S(1)}, f32[200]{0:T(256)}, u32[]{:S(2)}) copy-start(f32[200]{0:T(256)} %get-tuple-element.7) | copy-start | bytes 2404
  58.9 2.8 %copy-start.18 = (f32[200]{0:T(256)S(1)}, f32[200]{0:T(256)}, u32[]{:S(2)}) copy-start(f32[200]{0:T(256)} %get-tuple-element.8) | copy-start | bytes 2404
  59.1 2.9 %copy-start.46 = (f32[200]{0:T(256)S(1)}, f32[200]{0:T(256)}, u32[]{:S(2)}) copy-start(f32[200]{0:T(256)} %get-tuple-element.47) | copy-start | bytes 2404
  (32 other events, 83.3 us)
Sparse Core Ops, SparseCore 0:
  55.8 132.8 all-reduce.3
where the time goes:
time: 199 us; the launch traced here: 198 us
  waiting for transfers between devices  94.8 us (48%)
  blocking collectives  41.1 us (21%)
  other arithmetic  22.5 us (11%)
  between operations  14.8 us (7%)
  matrix products  10.1 us (5%)
  local copies, waits for them, and re-layouts  10 us (5%)
  starting transfers between devices  5.06 us (3%)
    psum x1, waiting for transfers between devices, body(): lax.psum((grad_expand, grad_reduce, grad_gain, grad_depthwise), ('ens', '...  85.5 us
    psum x1, blocking collectives, body(): lax.psum((grad_expand, grad_reduce, grad_gain, grad_depthwise), ('ens', '...  41.1 us
    reduce_sum x4, other arithmetic, depthwise_grad(): columns.append(jnp.sum(d_conv * window, axis=(1, 2)))  11.9 us
    reduce_sum x1, other arithmetic, cell_pass(): chan_mean = jnp.mean(conv_blk, axis=0, keepdims=True)  8.3 us
    unnamed x104, local copies, waits for them, and re-layouts  5.8 us
  transfers between devices with their start and end apart: 6, of which 5 were waited for; matrix products, arithmetic and copies ran while one was open for 3% of the time, Pallas kernels for 0%

commit v1 on v0

--- a/solution.py
+++ b/solution.py
@@ -1,8 +1,11 @@
+import functools
 import math
 
 import jax
 import jax.numpy as jnp
 from jax import lax
+from jax.experimental import pallas as pl
+from jax.experimental.pallas import tpu as pltpu
 from jax.sharding import PartitionSpec as P
 
 KS = 7
@@ -11,6 +14,246 @@
 norm_eps = 1e-06
 root_half = 0.7071067811865476
 gauss_norm = 0.3989422804014327
+
+
+MESH_AXES = ("ens", "lon", "lat")
+TILE = 16
+LANES = 128
+
+
+def bits_of(axis, size, first=0):
+    return [(axis, 1 << k, 2) for k in range(first, size.bit_length() - 1)]
+
+
+def make_streams(sizes):
+    lead = bits_of("lat", sizes["lat"])[:1]
+    groups = [bits_of("lat", sizes["lat"], 1), bits_of("lon", sizes["lon"])]
+    groups.append([("ens", 1, sizes["ens"])])
+    groups = [[digit for digit in group if digit[2] > 1] for group in groups]
+    streams = []
+    for turn in range(3):
+        order = groups[turn:] + groups[:turn]
+        streams.append(lead + [digit for group in order for digit in group])
+    return streams
+
+
+class Reducer:
+    def __init__(self, sizes, tiles_used):
+        self.streams = make_streams(sizes)
+        self.count = math.prod(sizes.values())
+        share = -(-tiles_used // len(self.streams))
+        self.share = -(-share // self.count) * self.count
+        self.tiles = self.share * len(self.streams)
+        self.copies = []
+        slots = []
+        for number, stages in enumerate(self.streams):
+            extent = self.share
+            place = number * self.share
+            for level, (axis, stride, radix) in enumerate(stages):
+                extent //= radix
+                for turn in range(1, radix):
+                    slots.append((number, level, turn, place))
+                    place += extent
+        self.slots = {(n, v, t): (i, p) for i, (n, v, t, p) in enumerate(slots)}
+
+    def scratch(self):
+        n = len(self.slots)
+        return [
+            pltpu.VMEM((2 * self.tiles, 8, LANES), jnp.float32),
+            pltpu.VMEM((self.tiles, TILE, LANES), jnp.bfloat16),
+            pltpu.VMEM((self.tiles, TILE, LANES), jnp.bfloat16),
+            pltpu.VMEM((self.tiles, TILE, LANES), jnp.bfloat16),
+            pltpu.SemaphoreType.DMA((n,)),
+            pltpu.SemaphoreType.DMA((n,)),
+            pltpu.SemaphoreType.DMA((n,)),
+            pltpu.SemaphoreType.DMA((n,)),
+        ]
+
+    def bind(self, acc, send, recv, full, ss, rs, sg, rg):
+        self.acc, self.send, self.recv, self.full = acc, send, recv, full
+        self.ss, self.rs, self.sg, self.rg = ss, rs, sg, rg
+        where = {axis: lax.axis_index(axis) for axis in MESH_AXES}
+        self.where = where
+        self.starts = []
+        self.extents = []
+        for number, stages in enumerate(self.streams):
+            start = number * self.share
+            extent = self.share
+            starts, extents = [start], [extent]
+            for axis, stride, radix in stages:
+                extent //= radix
+                start = start + lax.rem(lax.div(where[axis], stride), radix) * extent
+                starts.append(start)
+                extents.append(extent)
+            self.starts.append(starts)
+            self.extents.append(extents)
+        return self
+
+    def peer(self, digit, turn):
+        axis, stride, radix = digit
+        mine = lax.rem(lax.div(self.where[axis], stride), radix)
+        theirs = lax.rem(mine + turn, radix)
+        return theirs, {axis: self.where[axis] + (theirs - mine) * stride}
+
+    def peers(self):
+        seen = set()
+        found = []
+        for stages in self.streams:
+            for digit in stages:
+                for turn in range(1, digit[2]):
+                    if (digit, turn) not in seen:
+                        seen.add((digit, turn))
+                        found.append(self.peer(digit, turn)[1])
+        return found
+
+    def scatter_copy(self, number, level, turn):
+        digit = self.streams[number][level]
+        extent = self.extents[number][level + 1]
+        theirs, device = self.peer(digit, turn)
+        begin = self.starts[number][level] + theirs * extent
+        slot, place = self.slots[number, level, turn]
+        copy = pltpu.make_async_remote_copy(
+            src_ref=self.send.at[pl.ds(begin, extent)],
+            dst_ref=self.recv.at[pl.ds(place, extent)],
+            send_sem=self.ss.at[slot],
+            recv_sem=self.rs.at[slot],
+            device_id=device,
+            device_id_type=pl.DeviceIdType.MESH,
+        )
+        return copy, begin, extent, place
+
+    def scatter_start(self, number, level):
+        for turn in range(1, self.streams[number][level][2]):
+            copy, begin, extent, _ = self.scatter_copy(number, level, turn)
+            piece = self.acc[pl.ds(2 * begin, 2 * extent)].astype(jnp.bfloat16)
+            self.send[pl.ds(begin, extent)] = piece.reshape(extent, TILE, LANES)
+            copy.start()
+
+    def scatter_finish(self, number, level):
+        begin = self.starts[number][level + 1]
+        extent = self.extents[number][level + 1]
+        total = self.acc[pl.ds(2 * begin, 2 * extent)]
+        for turn in range(1, self.streams[number][level][2]):
+            copy, _, _, place = self.scatter_copy(number, level, turn)
+            copy.wait_recv()
+            piece = self.recv[pl.ds(place, extent)].astype(jnp.float32)
+            total = total + piece.reshape(2 * extent, 8, LANES)
+        self.acc[pl.ds(2 * begin, 2 * extent)] = total
+
+    def gather_copy(self, number, level, turn):
+        _, device = self.peer(self.streams[number][level], turn)
+        begin = self.starts[number][level + 1]
+        extent = self.extents[number][level + 1]
+        slot, _ = self.slots[number, level, turn]
+        block = self.full.at[pl.ds(begin, extent)]
+        return pltpu.make_async_remote_copy(
+            src_ref=block,
+            dst_ref=block,
+            send_sem=self.sg.at[slot],
+            recv_sem=self.rg.at[slot],
+            device_id=device,
+            device_id_type=pl.DeviceIdType.MESH,
+        )
+
+    def turns(self, number, level):
+        return range(1, self.streams[number][level][2])
+
+    def gather_start(self, number, level):
+        for turn in self.turns(number, level):
+            self.gather_copy(number, level, turn).start()
+
+    def gather_finish(self, number, level):
+        for turn in self.turns(number, level):
+            self.gather_copy(number, level, turn).wait_recv()
+
+    def scatter_first(self):
+        for number in range(len(self.streams)):
+            self.scatter_start(number, 0)
+
+    def run(self):
+        numbers = range(len(self.streams))
+        depth = len(self.streams[0])
+        for level in range(depth):
+            for number in numbers:
+                self.scatter_finish(number, level)
+                if level + 1 < depth:
+                    self.scatter_start(number, level + 1)
+                else:
+                    begin, extent = self.starts[number][-1], self.extents[number][-1]
+                    mine = self.acc[pl.ds(2 * begin, 2 * extent)].astype(jnp.bfloat16)
+                    self.full[pl.ds(begin, extent)] = mine.reshape(extent, TILE, LANES)
+                    self.gather_start(number, level)
+        for level in reversed(range(depth)):
+            for number in numbers:
+                self.gather_finish(number, level)
+                if level > 0:
+                    self.gather_start(number, level - 1)
+        for number in numbers:
+            for level in range(depth):
+                for turn in self.turns(number, level):
+                    self.scatter_copy(number, level, turn)[0].wait_send()
+                    self.gather_copy(number, level, turn).wait_send()
+
+
+def greet(devices):
+    barrier = pltpu.get_barrier_semaphore()
+    for device in devices:
+        pl.semaphore_signal(
+            barrier, inc=1, device_id=device, device_id_type=pl.DeviceIdType.MESH
+        )
+    pl.semaphore_wait(barrier, len(devices))
+
+
+def pack(acc, lane_tile, row_tile, block):
+    rows, width = block.shape
+    begin = lane_tile + row_tile
+    acc[begin : begin + rows // 8, :, :width] = block.reshape(rows // 8, 8, width)
+
+
+def reduce_kernel(reducer, scale, expand_ref, reduce_ref, small_ref, expand_out, reduce_out, small_out, *scratch):
+    channels, hidden = expand_ref.shape
+    eights = channels // 8
+    acc, full = scratch[0], scratch[3]
+    reducer.bind(*scratch)
+    spans = [(low, min(low + LANES, hidden)) for low in range(0, hidden, LANES)]
+    acc[...] = jnp.zeros_like(acc)
+    for at, (low, high) in enumerate(spans):
+        pack(acc, at * 2 * eights, 0, expand_ref[:, low:high] * scale)
+        pack(acc, at * 2 * eights, eights, reduce_ref[:, low:high] * scale)
+    pack(acc, len(spans) * 2 * eights, 0, small_ref[...] * scale)
+    greet(reducer.peers())
+    reducer.scatter_first()
+    reducer.run()
+    for at, (low, high) in enumerate(spans):
+        both = full[at * eights : (at + 1) * eights].astype(jnp.float32)
+        both = both.reshape(2 * channels, LANES)
+        expand_out[:, low:high] = both[:channels, : high - low]
+        reduce_out[low:high, :] = both[channels:].T[: high - low, :]
+    begin = len(spans) * eights
+    rest = full[begin : begin + -(-eights // 2)].astype(jnp.float32).reshape(-1, LANES)
+    small_out[...] = rest[:channels, : small_out.shape[1]]
+
+
+def all_reduce(sizes, scale, grad_expand, grad_reduce_t, small):
+    channels, hidden = grad_expand.shape
+    eights = channels // 8
+    tiles = -(-hidden // LANES) * eights + -(-eights // 2)
+    reducer = Reducer(sizes, tiles)
+    vmem = pl.BlockSpec(memory_space=pltpu.VMEM)
+    return pl.pallas_call(
+        functools.partial(reduce_kernel, reducer, scale),
+        out_shape=(
+            jax.ShapeDtypeStruct((channels, hidden), jnp.float32),
+            jax.ShapeDtypeStruct((hidden, channels), jnp.float32),
+            jax.ShapeDtypeStruct(small.shape, jnp.float32),
+        ),
+        in_specs=[vmem] * 3,
+        out_specs=[vmem] * 3,
+        scratch_shapes=reducer.scratch(),
+        compiler_params=pltpu.CompilerParams(
+            collective_id=0, has_side_effects=True, vmem_limit_bytes=56 * 1024 * 1024
+        ),
+    )(grad_expand, grad_reduce_t, small)
 
 
 def with_halo(cells, sides, width):
@@ -70,7 +313,7 @@
     gelu_slope = normal_cdf + pre_act * normal_pdf
     branch = jnp.dot(reduce_weight.T, hidden, preferred_element_type=jnp.float32)
     out_blk = ((state_blk.astype(jnp.float32) + branch) * mask_blk[None, :]).astype(jnp.bfloat16)
-    grad_reduce = jnp.dot(hidden, cot_blk.T, preferred_element_type=jnp.float32)
+    grad_reduce = jnp.dot(cot_blk, hidden.T, preferred_element_type=jnp.float32)
     d_hidden = jnp.dot(reduce_weight, cot_blk, preferred_element_type=jnp.float32)
     d_pre = (d_hidden * gelu_slope).astype(jnp.bfloat16)
     grad_expand = jnp.dot(scaled, d_pre.T, preferred_element_type=jnp.float32)
@@ -122,13 +365,12 @@
         d_conv.reshape(channels, tile_rows, tile_cols), padded, tile_rows, tile_cols
     )
     grad_scale = 1.0 / math.sqrt(lax.axis_size("ens") * lat_count * lon_count * cell_count)
-    grad_expand = grad_expand * grad_scale
-    grad_reduce = grad_reduce * grad_scale
-    grad_gain = grad_gain * grad_scale
-    grad_depthwise = grad_depthwise * grad_scale
-    grad_expand, grad_reduce, grad_gain, grad_depthwise = lax.psum(
-        (grad_expand, grad_reduce, grad_gain, grad_depthwise), ("ens", "lon", "lat")
-    )
+    sizes = {axis: lax.axis_size(axis) for axis in MESH_AXES}
+    small = jnp.concatenate([grad_depthwise, grad_gain[:, None]], axis=1)
+    grad_expand, grad_reduce, small = all_reduce(
+        sizes, grad_scale, grad_expand, grad_reduce, small
+    )
+    grad_depthwise, grad_gain = small[:, :-1], small[:, -1]
     next_state = out_flat.reshape(channels, tile_rows, tile_cols)[None]
     return (next_state, grad_depthwise, grad_gain, grad_expand, grad_reduce)
 

time: 199 us -> 139 us (0.70)
  waiting for transfers between devices: 94.8 us -> 9.27 us
  local copies, waits for them, and re-layouts: 10 us -> 59.2 us
  blocking collectives: 41.1 us -> 0 us
  Pallas kernels: 0 us -> 31 us
  between operations: 14.8 us -> 1.19 us
    psum x1 -> x0, waiting for transfers between devices: 85.5 us -> none  [body(): lax.psum((grad_expand, grad_reduce, grad_gain, grad_depthwise), ('ens', '...]
    psum x1 -> x0, blocking collectives: 41.1 us -> none  [body(): lax.psum((grad_expand, grad_reduce, grad_gain, grad_depthwise), ('ens', '...]
    another operation x1 -> x49, local copies, waits for them, and re-layouts: 0.17 us -> 38.7 us  [depthwise_grad(): return jnp.stack(columns, axis=1)]
    pallas_call x0 -> x1, Pallas kernels: none -> 31 us  [all_reduce(): pl.pallas_call(functools.partial(reduce_kernel, reducer, scale), out_shap...]
    concatenate x0 -> x1, local copies, waits for them, and re-layouts: none -> 5.77 us  [body(): small = jnp.concatenate([grad_depthwise, grad_gain[:, None]], axis=1)]
    unnamed x104 -> x47, local copies, waits for them, and re-layouts: 5.8 us -> 7.48 us
  transfers between devices with their start and end apart: 6 -> 5, of which waited for: 5 -> 4; matrix products, arithmetic and copies ran while one was open for 3% -> 1% of each run, Pallas kernels for 0% -> 0%
where the time goes in v1:
time: 139 us; the launch traced here: 138 us
  local copies, waits for them, and re-layouts  59.2 us (43%)
  Pallas kernels  31 us (22%)
  other arithmetic  23.2 us (17%)
  waiting for transfers between devices  9.27 us (7%)
  matrix products  9.15 us (7%)
  starting transfers between devices  5.02 us (4%)
    another operation x49, local copies, waits for them, and re-layouts, depthwise_grad(): return jnp.stack(columns, axis=1)  38.7 us
    pallas_call x1, Pallas kernels, all_reduce(): pl.pallas_call(functools.partial(reduce_kernel, reducer, scale), out_shap...  31 us
    reduce_sum x4, other arithmetic, depthwise_grad(): columns.append(jnp.sum(d_conv * window, axis=(1, 2)))  12.6 us
    reduce_sum x1, other arithmetic, cell_pass(): chan_mean = jnp.mean(conv_blk, axis=0, keepdims=True)  8.26 us
    unnamed x47, local copies, waits for them, and re-layouts  7.48 us
    concatenate x1, local copies, waits for them, and re-layouts, body(): small = jnp.concatenate([grad_depthwise, grad_gain[:, None]], axis=1)  5.77 us
    ppermute x2, waiting for transfers between devices, with_halo(): lax.ppermute(tail, axis, [(i, (i + 1) % count) for i in range(count)])  3.92 us
    ppermute x1, waiting for transfers between devices, swapped(): lax.ppermute(array, axis, [(i, i ^ 1 << stride) for i in range(lax.axis_s...  3.33 us
  transfers between devices with their start and end apart: 5, of which 4 were waited for; matrix products, arithmetic and copies ran while one was open for 1% of the time, Pallas kernels for 0%

profile of v1, /device:TPU:0, one launch (start us, length us, event | category | flops | bytes accessed | tf_op | source)
XLA Modules:
  0.0 138.1 jit_solution(5961808649393315654)
XLA Ops:
  3.5 3.0 %collective-permute-start = (bf16[200,8,3]{0,2,1:T(4,128)(2,1)S(1)}, bf16[200,8,3]{0,2,1:T(4,128)(2,1)S(1)}, u32[]{:S(2)}, u32[]{:S(2)}) collective-permute-start(bf16[200,8,3]{0,2,1:T(4,128)(2,1)S(1)} %get-tuple-element.97), channel_id=1, source_target_pairs={{0,4},{4,0},{1,5},{5,1},{2,6},{6,2},{3,7},{7,3},{8,12},{12,8},{9,1... | collective-permute-start | bytes 28808 | tf_op jit(solution)/shard_map/ppermute | solution.py:266
  6.7 1.6 %collective-permute-done = bf16[200,8,3]{0,2,1:T(4,128)(2,1)S(1)} collective-permute-done((bf16[200,8,3]{0,2,1:T(4,128)(2,1)S(1)}, bf16[200,8,3]{0,2,1:T(4,128)(2,1)S(1)}, u32[]{:S(2)}, u32[]{:S(2)}) %collective-permute-start) | collective-permute-done | bytes 9632 | tf_op jit(solution)/shard_map/ppermute | solution.py:266
  8.3 2.0 %collective-permute-done.1 = bf16[200,8,3]{0,2,1:T(4,128)(2,1)S(1)} collective-permute-done((bf16[200,8,3]{0,2,1:T(4,128)(2,1)S(1)}, bf16[200,8,3]{0,2,1:T(4,128)(2,1)S(1)}, u32[]{:S(2)}, u32[]{:S(2)}) %collective-permute-start.1) | collective-permute-done | bytes 9632 | tf_op jit(solution)/shard_map/ppermute | solution.py:268
  11.7 1.6 %collective-permute-start.4 = (bf16[200,3,134]{0,2,1:T(8,128)(2,1)S(1)}, bf16[200,3,134]{0,2,1:T(8,128)(2,1)S(1)}, u32[]{:S(2)}, u32[]{:S(2)}) collective-permute-start(bf16[200,3,134]{0,2,1:T(8,128)(2,1)S(1)} %get-tuple-element.95), channel_id=1, source_target_pairs={{1,0},{2,1},{3,2},{0,3},{5,4},{6,5},{7,6},{4,7},{9,8},{10,9},{11,1... | collective-permute-start | bytes 482408 | tf_op jit(solution)/shard_map/ppermute | solution.py:268
  13.4 2.3 %collective-permute-done.2 = bf16[200,3,134]{0,2,1:T(8,128)(2,1)S(1)} collective-permute-done((bf16[200,3,134]{0,2,1:T(8,128)(2,1)S(1)}, bf16[200,3,134]{0,2,1:T(8,128)(2,1)S(1)}, u32[]{:S(2)}, u32[]{:S(2)}) %collective-permute-start.2) | collective-permute-done | bytes 160832 | tf_op jit(solution)/shard_map/ppermute | solution.py:266
  15.7 3.3 %collective-permute-done.3 = bf16[200,3,134]{0,2,1:T(8,128)(2,1)S(1)} collective-permute-done((bf16[200,3,134]{0,2,1:T(8,128)(2,1)S(1)}, bf16[200,3,134]{0,2,1:T(8,128)(2,1)S(1)}, u32[]{:S(2)}, u32[]{:S(2)}) %collective-permute-start.3) | collective-permute-done | bytes 160832 | tf_op jit(solution)/shard_map/ppermute | solution.py:276
  19.3 8.3 %fusion.120 = (f32[8,128]{1,0:T(8,128)S(1)}, f32[200,8,128]{0,2,1:T(8,128)S(1)}) fusion(bf16[200,11,134]{0,2,1:T(8,128)(2,1)S(1)} %get-tuple-element.94, f32[200]{0:T(256)S(1)} %bitcast.308, f32[200]{0:T(256)S(1)} %bitcast.309, f32[200]{0:T(256)S(1)} %bitcast.262, f32[200]{0:T(256)S(1)} %bitcast.263, f32[200]{0:T(256)S(1)} %bitcast.264, ...), kind=kLoop, calls=%fused_computation.251 | loop fusion | flops 33790976 | bytes 18494496 | tf_op jit(solution)/shard_map/reduce_sum | solution.py:303
  28.6 1.5 %copy.168 = f32[200,1024]{1,0:T(8,128)S(1)} copy(f32[200,1024]{0,1:T(8,128)} %bitcast.214) | data formatting | bytes 1638400 | tf_op jit(solution)/shard_map/reshape | solution.py:356
  30.2 2.2 %fusion.9 = (bf16[800,1024]{1,0:T(8,128)(2,1)}, f32[1024,800]{0,1:T(8,128)S(1)}) fusion(bf16[200,800]{1,0:T(8,128)(2,1)S(1)} %copy-done, f32[200,1024]{1,0:T(8,128)S(1)} %copy.168, f32[200]{0:T(256)S(1)} %copy-done.11, f32[1024]{0:T(1024)S(1)} %rsqrt_bitcast_fusion, f32[1024]{0:T(1024)S(1)} %get-tuple-element.150), kind=kOutput, calls=%fused_computation.12 | convolution fusion | flops 332595200 | bytes 6063392 | tf_op jit(solution)/shard_map/dot_general | solution.py:309
  32.4 1.7 %fusion.5 = bf16[800,1024]{1,0:T(8,128)(2,1)S(1)} fusion(f32[1024,800]{0,1:T(8,128)S(1)} %get-tuple-element.153, bf16[800,200]{0,1:T(8,128)(2,1)S(1)} %copy-done.19, bf16[25,8,8,128]{3,2,1,0:T(8,128)(2,1)S(1)} %bitcast.217, bf16[1024]{0:T(1024)(128)(2,1)S(1)} %bitcast.221), kind=kOutput, calls=%fused_computation.6 | convolution fusion | flops 336076800 | bytes 5646848 | tf_op jit(solution)/shard_map/dot_general | solution.py:317
  34.0 1.7 %fusion.118.expand_ref = f32[200,800]{1,0:T(8,128)} fusion(bf16[800,1024]{1,0:T(8,128)(2,1)S(1)} %fusion.5, f32[200,1024]{1,0:T(8,128)S(1)} %copy.168, f32[200]{0:T(256)S(1)} %copy-done.11, f32[1024]{0:T(1024)S(1)} %rsqrt_bitcast_fusion, f32[1024]{0:T(1024)S(1)} %get-tuple-element.150), kind=kOutput, calls=%fused_computation.249 | convolution fusion | flops 328499200 | bytes 3106592 | tf_op jit(solution)/shard_map/dot_general | solution.py:319
  37.1 1.9 %multiply_reduce_fusion.2 = (f32[200]{0:T(256)}, f32[200,1024]{1,0:T(8,128)}) fusion(bf16[25,8,8,128]{3,2,1,0:T(8,128)(2,1)S(1)} %bitcast.215, bf16[1024]{0:T(1024)(128)(2,1)S(1)} %bitcast.222, f32[1024]{0:T(1024)S(1)} %get-tuple-element.155, f32[200,1024]{1,0:T(8,128)S(1)} %copy.168, f32[1024]{0:T(1024)S(1)} %get-tuple-element.150, ...), kind=kLoop, calls=%fused_computation.213 | loop fusion | flops 2252600 | bytes 2887232 | tf_op jit(solution)/shard_map/reduce_sum | solution.py:298
  39.0 1.5 %copy.169 = f32[200,1024]{0,1:T(8,128)S(1)} copy(f32[200,1024]{1,0:T(8,128)} %get-tuple-element.90) | data formatting | bytes 1638400 | tf_op jit(solution)/shard_map/reshape | solution.py:365
  40.4 3.8 %fusion.59 = (f32[200]{0:T(256)}, f32[200]{0:T(256)}, f32[200]{0:T(256)}, f32[200]{0:T(256)S(1)}, f32[200]{0:T(256)S(1)}, /*index=5*/f32[200]{0:T(256)S(1)}, f32...) fusion(bf16[200,11,134]{0,2,1:T(8,128)(2,1)S(1)} %get-tuple-ele, ...), kind=kLoop, calls=%fused_computation.160 | loop fusion | flops 11055600 | bytes 8206400 | tf_op jit(solution)/shard_map/reduce_sum | solution.py:298
  44.2 3.8 %fusion.109 = (f32[200]{0:T(256)}, f32[200]{0:T(256)}, f32[200]{0:T(256)}, f32[200]{0:T(256)}, f32[200]{0:T(256)}, /*index=5*/f32[200]{0:T(256)}, f32[200]{0:T(2...) fusion(bf16[200,11,134]{0,2,1:T(8,128)(2,1)S(1)} %get-tuple-ele, ...), kind=kLoop, calls=%fused_computation.210 | loop fusion | flops 11055600 | bytes 8206400 | tf_op jit(solution)/shard_map/reduce_sum | solution.py:298
  48.0 1.6 %fusion.114.reduce_ref = f32[200,800]{1,0:T(8,128)} fusion(bf16[800,1024]{1,0:T(8,128)(2,1)S(1)} %copy-done.2, bf16[25,8,8,128]{3,2,1,0:T(8,128)(2,1)S(1)} %bitcast.218, bf16[1024]{0:T(1024)(128)(2,1)S(1)} %bitcast.223), kind=kOutput, calls=%fused_computation.234 | convolution fusion | flops 327884800 | bytes 2690048 | tf_op jit(solution)/shard_map/dot_general | solution.py:316
  53.3 3.2 %fusion.91 = (f32[200]{0:T(256)}, f32[200]{0:T(256)}, f32[200]{0:T(256)}, f32[200]{0:T(256)}, f32[200]{0:T(256)}, /*index=5*/f32[200]{0:T(256)}, f32[200]{0:T(25...) fusion(bf16[200,11,134]{0,2,1:T(8,128)(2,1)S(1)} %get-tuple-element.94, ...), kind=kLoop, calls=%fused_computation.192 | loop fusion | flops 11056800 | bytes 3715200 | tf_op jit(solution)/shard_map/reduce_sum | solution.py:298
  80.9 1.5 %copy.158 = f32[200,1]{1,0:T(8,128)} copy(f32[200,1]{0,1:T(1,128)} %bitcast.235) | data formatting | bytes 1600 | tf_op jit(solution)/shard_map/stack | solution.py:299
  89.5 1.4 %copy.152 = f32[200,1]{1,0:T(8,128)} copy(f32[200,1]{0,1:T(1,128)} %bitcast.229) | data formatting | bytes 1600 | tf_op jit(solution)/shard_map/stack | solution.py:299
  94.8 5.8 %concatenate.68.small_ref = f32[200,50]{1,0:T(8,128)} concatenate(f32[200,1]{1,0:T(8,128)S(1)} %copy.116, f32[200,1]{1,0:T(8,128)S(1)} %copy.117, f32[200,1]{1,0:T(8,128)S(1)} %copy.118, f32[200,1]{1,0:T(8,128)} %copy.119, f32[200,1]{1,0:T(8,128)} %copy.120, f32[200,1]{1,0:T(8,128)} %copy.121, f32[200,1]{1,0:T(8,128)S(1)} %copy.122, f32[200,1]{1,0:T(8,128)S(1)} %copy.123, ...), dimensions={1} | concatenate | bytes 80000 | tf_op jit(solution)/shard_map/concatenate | solution.py:369
  100.6 31.0 %shard_map.110 = (f32[200,800]{1,0:T(8,128)}, f32[800,200]{1,0:T(8,128)}, f32[200,50]{1,0:T(8,128)}) custom-call(f32[200,800]{1,0:T(8,128)} %fusion.118.expand_ref, f32[200,800]{1,0:T(8,128)} %fusion.114.reduce_ref, f32[200,50]{1,0:T(8,128)} %concatenate.68.small_ref), custom_call_target="tpu_custom_call" | custom-call | tf_op jit(solution)/shard_map/pallas_call | solution.py:243
  131.6 1.7 %slice_reduce_fusion = f32[200]{0:T(256)} fusion(f32[200,50]{1,0:T(8,128)} %get-tuple-element.8), kind=kLoop, calls=%fused_computation.242 | loop fusion | bytes 1600 | tf_op jit(solution)/shard_map/slice | solution.py:373
  133.3 1.6 %copy.166 = f32[200,49]{0,1:T(8,128)} copy(f32[200,49]{1,0:T(8,128)} %bitcast.220) | data formatting | bytes 78400
  134.9 2.3 %copy.167 = f32[800,200]{0,1:T(8,128)} copy(f32[800,200]{1,0:T(8,128)} %get-tuple-element.25) | data formatting | bytes 1280000
  (114 shorter events, 46.6 us)
Async XLA Ops:
  0.6 29.5 %copy-start = (bf16[200,800]{1,0:T(8,128)(2,1)S(1)}, bf16[200,800]{1,0:T(8,128)(2,1)}, u32[]{:S(2)}) copy-start(bf16[200,800]{1,0:T(8,128)(2,1)} %param.11) | copy-start | bytes 960004
  0.6 6.0 %copy-start.10 = (f32[200,49]{0,1:T(8,128)S(1)}, f32[200,49]{0,1:T(8,128)}, u32[]{:S(2)}) copy-start(f32[200,49]{0,1:T(8,128)} %param.9) | copy-start | bytes 117604
  3.5 4.8 %collective-permute-start = (bf16[200,8,3]{0,2,1:T(4,128)(2,1)S(1)}, bf16[200,8,3]{0,2,1:T(4,128)(2,1)S(1)}, u32[]{:S(2)}, u32[]{:S(2)}) collective-permute-start(bf16[200,8,3]{0,2,1:T(4,128)(2,1)S(1)} %get-tuple-element.97), channel_id=1, source_target_pairs={{0,4},{4,0},{1,5},{5,1},{2,6},{6,2},{3,7},{7,3},{8,12},{12,8},{9,1... | collective-permute-start | bytes 28808 | tf_op jit(solution)/shard_map/ppermute | solution.py:266
  6.5 3.7 %collective-permute-start.1 = (bf16[200,8,3]{0,2,1:T(4,128)(2,1)S(1)}, bf16[200,8,3]{0,2,1:T(4,128)(2,1)S(1)}, u32[]{:S(2)}, u32[]{:S(2)}) collective-permute-start(bf16[200,8,3]{0,2,1:T(4,128)(2,1)S(1)} %get-tuple-element.98), channel_id=1, source_target_pairs={{4,0},{0,4},{5,1},{1,5},{6,2},{2,6},{7,3},{3,7},{12,8},{8,12},{13,... | collective-permute-start | bytes 28808 | tf_op jit(solution)/shard_map/ppermute | solution.py:268
  10.4 5.3 %collective-permute-start.2 = (bf16[200,3,134]{0,2,1:T(8,128)(2,1)S(1)}, bf16[200,3,134]{0,2,1:T(8,128)(2,1)S(1)}, u32[]{:S(2)}, u32[]{:S(2)}) collective-permute-start(bf16[200,3,134]{0,2,1:T(8,128)(2,1)S(1)} %get-tuple-element.96), channel_id=1, source_target_pairs={{0,1},{1,2},{2,3},{3,0},{4,5},{5,6},{6,7},{7,4},{8,9},{9,10},{10,1... | collective-permute-start | bytes 482408 | tf_op jit(solution)/shard_map/ppermute | solution.py:266
  11.5 7.5 %collective-permute-start.3 = (bf16[200,3,134]{0,2,1:T(8,128)(2,1)S(1)}, bf16[200,3,134]{0,2,1:T(8,128)(2,1)S(1)}, u32[]{:S(2)}, u32[]{:S(2)}) collective-permute-start(bf16[200,3,134]{0,2,1:T(8,128)(2,1)S(1)} %rev.3), channel_id=1, source_target_pairs={{0,4},{4,0},{1,5},{5,1},{2,6},{6,2},{3,7},{7,3},{8,12},{12,8},{9,1... | collective-permute-start | bytes 482408 | tf_op jit(solution)/shard_map/ppermute | solution.py:276
  11.7 7.3 %collective-permute-start.4 = (bf16[200,3,134]{0,2,1:T(8,128)(2,1)S(1)}, bf16[200,3,134]{0,2,1:T(8,128)(2,1)S(1)}, u32[]{:S(2)}, u32[]{:S(2)}) collective-permute-start(bf16[200,3,134]{0,2,1:T(8,128)(2,1)S(1)} %get-tuple-element.95), channel_id=1, source_target_pairs={{1,0},{2,1},{3,2},{0,3},{5,4},{6,5},{7,6},{4,7},{9,8},{10,9},{11,1... | collective-permute-start | bytes 482408 | tf_op jit(solution)/shard_map/ppermute | solution.py:268
  27.6 2.5 %copy-start.11 = (f32[200]{0:T(256)S(1)}, f32[200]{0:T(256)}, u32[]{:S(2)}) copy-start(f32[200]{0:T(256)} %param.10) | copy-start | bytes 2404
  30.1 2.2 %copy-start.6 = (bf16[1,200,8,128]{3,2,1,0:T(8,128)(2,1)S(1)}, bf16[1,200,8,128]{3,2,1,0:T(8,128)(2,1)}, u32[]{:S(2)}) copy-start(bf16[1,200,8,128]{3,2,1,0:T(8,128)(2,1)} %param.13) | copy-start | bytes 1228804
  30.2 2.2 %copy-start.19 = (bf16[800,200]{0,1:T(8,128)(2,1)S(1)}, bf16[800,200]{0,1:T(8,128)(2,1)}, u32[]{:S(2)}) copy-start(bf16[800,200]{0,1:T(8,128)(2,1)} %param.12) | copy-start | bytes 960004
  44.2 3.8 %copy-start.2 = (bf16[800,1024]{1,0:T(8,128)(2,1)S(1)}, bf16[800,1024]{1,0:T(8,128)(2,1)}, u32[]{:S(2)}) copy-start(bf16[800,1024]{1,0:T(8,128)(2,1)} %get-tuple-element.152) | copy-start | bytes 4915204
  44.2 3.8 %copy-start.7 = (bf16[1,200,8,128]{3,2,1,0:T(8,128)(2,1)S(1)}, bf16[1,200,8,128]{3,2,1,0:T(8,128)(2,1)}, u32[]{:S(2)}) copy-start(bf16[1,200,8,128]{3,2,1,0:T(8,128)(2,1)} %param.13) | copy-start | bytes 1228804
  48.0 1.6 %copy-start.4 = (bf16[1,200,8,128]{3,2,1,0:T(8,128)(2,1)S(1)}, bf16[1,200,8,128]{3,2,1,0:T(8,128)(2,1)}, u32[]{:S(2)}) copy-start(bf16[1,200,8,128]{3,2,1,0:T(8,128)(2,1)} %param.7) | copy-start | bytes 1228804
  48.0 1.6 %copy-start.18 = (f32[1024]{0:T(1024)S(1)}, f32[1024]{0:T(1024)}, u32[]{:S(2)}) copy-start(f32[1024]{0:T(1024)} %get-tuple-element.148) | copy-start | bytes 12292
  48.0 1.6 %copy-start.20 = (bf16[800,200]{0,1:T(8,128)(2,1)S(1)}, bf16[800,200]{0,1:T(8,128)(2,1)}, u32[]{:S(2)}) copy-start(bf16[800,200]{0,1:T(8,128)(2,1)} %param.12) | copy-start | bytes 960004
  49.6 1.4 %copy-start.17 = (f32[200]{0:T(256)S(1)}, f32[200]{0:T(256)}, u32[]{:S(2)}) copy-start(f32[200]{0:T(256)} %get-tuple-element.89) | copy-start | bytes 2404
  53.3 5.6 %copy-start.16 = (f32[200]{0:T(256)S(1)}, f32[200]{0:T(256)}, u32[]{:S(2)}) copy-start(f32[200]{0:T(256)} %get-tuple-element.47) | copy-start | bytes 2404
  56.5 12.0 %copy-start.15 = (f32[200]{0:T(256)S(1)}, f32[200]{0:T(256)}, u32[]{:S(2)}) copy-start(f32[200]{0:T(256)} %get-tuple-element.49) | copy-start | bytes 2404
  65.3 25.6 %copy-start.14 = (f32[200]{0:T(256)S(1)}, f32[200]{0:T(256)}, u32[]{:S(2)}) copy-start(f32[200]{0:T(256)} %get-tuple-element.39) | copy-start | bytes 2404
  66.1 25.6 %copy-start.13 = (f32[200]{0:T(256)S(1)}, f32[200]{0:T(256)}, u32[]{:S(2)}) copy-start(f32[200]{0:T(256)} %get-tuple-element.40) | copy-start | bytes 2404
  66.9 25.6 %copy-start.12 = (f32[200]{0:T(256)S(1)}, f32[200]{0:T(256)}, u32[]{:S(2)}) copy-start(f32[200]{0:T(256)} %get-tuple-element.41) | copy-start | bytes 2404
  68.7 26.1 %copy-start.8 = (f32[200,1]{1,0:T(8,128)S(1)}, f32[200,1]{1,0:T(8,128)}, u32[]{:S(2)}) copy-start(f32[200,1]{1,0:T(8,128)} %copy.140) | copy-start | bytes 2404
  68.7 26.1 %copy-start.9 = (f32[200,1]{1,0:T(8,128)S(1)}, f32[200,1]{1,0:T(8,128)}, u32[]{:S(2)}) copy-start(f32[200,1]{1,0:T(8,128)} %copy.165) | copy-start | bytes 2404
  131.6 5.6 %copy-start.5 = (f32[200,800]{1,0:T(8,128)S(1)}, f32[200,800]{1,0:T(8,128)}, u32[]{:S(2)}) copy-start(f32[200,800]{1,0:T(8,128)} %get-tuple-element.165) | copy-start | bytes 1920004
  (2 other events, 2.4 us)

commit v2 on v1

--- a/solution.py
+++ b/solution.py
@@ -25,7 +25,7 @@
     return [(axis, 1 << k, 2) for k in range(first, size.bit_length() - 1)]
 
 
-def make_streams(sizes):
+def big_streams(sizes):
     lead = bits_of("lat", sizes["lat"])[:1]
     groups = [bits_of("lat", sizes["lat"], 1), bits_of("lon", sizes["lon"])]
     groups.append([("ens", 1, sizes["ens"])])
@@ -37,14 +37,21 @@
     return streams
 
 
+def small_streams(sizes):
+    stages = []
+    for axis in ("lat", "lon", "ens"):
+        whole = [(axis, 1, sizes[axis])] if sizes[axis] <= 4 else bits_of(axis, sizes[axis])
+        stages += [digit for digit in whole if digit[2] > 1]
+    return [stages]
+
+
 class Reducer:
-    def __init__(self, sizes, tiles_used):
-        self.streams = make_streams(sizes)
+    def __init__(self, sizes, streams, tiles_used):
+        self.streams = streams
         self.count = math.prod(sizes.values())
         share = -(-tiles_used // len(self.streams))
         self.share = -(-share // self.count) * self.count
         self.tiles = self.share * len(self.streams)
-        self.copies = []
         slots = []
         for number, stages in enumerate(self.streams):
             extent = self.share
@@ -166,13 +173,15 @@
         for turn in self.turns(number, level):
             self.gather_copy(number, level, turn).wait_recv()
 
-    def scatter_first(self):
-        for number in range(len(self.streams)):
-            self.scatter_start(number, 0)
-
-    def run(self):
+    def clear(self):
+        self.acc[...] = jnp.zeros_like(self.acc)
+
+    def steps(self):
         numbers = range(len(self.streams))
         depth = len(self.streams[0])
+        for number in numbers:
+            self.scatter_start(number, 0)
+        yield True
         for level in range(depth):
             for number in numbers:
                 self.scatter_finish(number, level)
@@ -183,11 +192,13 @@
                     mine = self.acc[pl.ds(2 * begin, 2 * extent)].astype(jnp.bfloat16)
                     self.full[pl.ds(begin, extent)] = mine.reshape(extent, TILE, LANES)
                     self.gather_start(number, level)
+            yield True
         for level in reversed(range(depth)):
             for number in numbers:
                 self.gather_finish(number, level)
                 if level > 0:
                     self.gather_start(number, level - 1)
+            yield True
         for number in numbers:
             for level in range(depth):
                 for turn in self.turns(number, level):
@@ -195,65 +206,10 @@
                     self.gather_copy(number, level, turn).wait_send()
 
 
-def greet(devices):
-    barrier = pltpu.get_barrier_semaphore()
-    for device in devices:
-        pl.semaphore_signal(
-            barrier, inc=1, device_id=device, device_id_type=pl.DeviceIdType.MESH
-        )
-    pl.semaphore_wait(barrier, len(devices))
-
-
 def pack(acc, lane_tile, row_tile, block):
     rows, width = block.shape
     begin = lane_tile + row_tile
     acc[begin : begin + rows // 8, :, :width] = block.reshape(rows // 8, 8, width)
-
-
-def reduce_kernel(reducer, scale, expand_ref, reduce_ref, small_ref, expand_out, reduce_out, small_out, *scratch):
-    channels, hidden = expand_ref.shape
-    eights = channels // 8
-    acc, full = scratch[0], scratch[3]
-    reducer.bind(*scratch)
-    spans = [(low, min(low + LANES, hidden)) for low in range(0, hidden, LANES)]
-    acc[...] = jnp.zeros_like(acc)
-    for at, (low, high) in enumerate(spans):
-        pack(acc, at * 2 * eights, 0, expand_ref[:, low:high] * scale)
-        pack(acc, at * 2 * eights, eights, reduce_ref[:, low:high] * scale)
-    pack(acc, len(spans) * 2 * eights, 0, small_ref[...] * scale)
-    greet(reducer.peers())
-    reducer.scatter_first()
-    reducer.run()
-    for at, (low, high) in enumerate(spans):
-        both = full[at * eights : (at + 1) * eights].astype(jnp.float32)
-        both = both.reshape(2 * channels, LANES)
-        expand_out[:, low:high] = both[:channels, : high - low]
-        reduce_out[low:high, :] = both[channels:].T[: high - low, :]
-    begin = len(spans) * eights
-    rest = full[begin : begin + -(-eights // 2)].astype(jnp.float32).reshape(-1, LANES)
-    small_out[...] = rest[:channels, : small_out.shape[1]]
-
-
-def all_reduce(sizes, scale, grad_expand, grad_reduce_t, small):
-    channels, hidden = grad_expand.shape
-    eights = channels // 8
-    tiles = -(-hidden // LANES) * eights + -(-eights // 2)
-    reducer = Reducer(sizes, tiles)
-    vmem = pl.BlockSpec(memory_space=pltpu.VMEM)
-    return pl.pallas_call(
-        functools.partial(reduce_kernel, reducer, scale),
-        out_shape=(
-            jax.ShapeDtypeStruct((channels, hidden), jnp.float32),
-            jax.ShapeDtypeStruct((hidden, channels), jnp.float32),
-            jax.ShapeDtypeStruct(small.shape, jnp.float32),
-        ),
-        in_specs=[vmem] * 3,
-        out_specs=[vmem] * 3,
-        scratch_shapes=reducer.scratch(),
-        compiler_params=pltpu.CompilerParams(
-            collective_id=0, has_side_effects=True, vmem_limit_bytes=56 * 1024 * 1024
-        ),
-    )(grad_expand, grad_reduce_t, small)
 
 
 def with_halo(cells, sides, width):
@@ -276,63 +232,212 @@
     return lax.ppermute(array, axis, [(i, i ^ 1 << stride) for i in range(lax.axis_size(axis))])
 
 
-def depthwise(padded, dw_weight, out_rows, out_cols):
-    conv_sum = jnp.zeros((padded.shape[0], out_rows, out_cols), jnp.float32)
-    for shift_a in range(KS):
+def lane_spans(width):
+    return [(low, min(low + LANES, width)) for low in range(0, width, LANES)]
+
+
+def window(main, edge, lane, shift):
+    width = main.shape[1]
+    if shift == 0:
+        return main
+    outside = lane < shift if shift > 0 else lane >= width + shift
+    return pltpu.roll(jnp.where(outside, edge, main), (-shift) % width, 1)
+
+
+def block_kernel(
+    big,
+    small,
+    scale,
+    main_ref,
+    edge_ref,
+    cot_ref,
+    mask_ref,
+    dw_ref,
+    gain_ref,
+    expand_ref,
+    reduce_ref,
+    state_out,
+    expand_out,
+    reduce_out,
+    small_out,
+    expand_t,
+    reduce_t,
+    conv,
+    scaled_all,
+    hidden_all,
+    d_pre_all,
+    gain_sum,
+    *scratch,
+):
+    channels, hidden_units = expand_ref.shape
+    eights = channels // 8
+    margin = KS // 2
+    tile_rows = main_ref.shape[0] - 2 * margin
+    width = main_ref.shape[2]
+    spans = lane_spans(hidden_units)
+    big.bind(*scratch[:8])
+    small.bind(*scratch[8:])
+    peers = big.peers() + small.peers()
+    barrier_count = len(peers)
+    barrier = pltpu.get_barrier_semaphore()
+    for device in peers:
+        pl.semaphore_signal(
+            barrier, inc=1, device_id=device, device_id_type=pl.DeviceIdType.MESH
+        )
+    big.clear()
+    small.clear()
+    gain_sum[...] = jnp.zeros_like(gain_sum)
+    for low, high in spans:
+        piece = expand_ref[:, low:high].astype(jnp.float32).T
+        expand_t[low:high, :] = piece.astype(jnp.bfloat16)
+        piece = reduce_ref[low:high, :].astype(jnp.float32).T
+        reduce_t[:, low:high] = piece.astype(jnp.bfloat16)
+    lane = lax.broadcasted_iota(jnp.int32, (8, width), 1)
+
+    def conv_step(step, carry):
+        rows = pl.ds(pl.multiple_of(step * 8, 8), 8)
+        taps = dw_ref[rows, :]
+        sums = [jnp.zeros((8, width), jnp.float32) for _ in range(tile_rows)]
         for shift_b in range(KS):
-            tap_weight = dw_weight[:, shift_a * KS + shift_b][:, None, None]
-            window = padded[:, shift_a : shift_a + out_rows, shift_b : shift_b + out_cols].astype(
-                jnp.float32
-            )
-            conv_sum = conv_sum + tap_weight * window
-    return conv_sum
-
-
-def depthwise_grad(d_conv, padded, out_rows, out_cols):
-    columns = []
-    for shift_a in range(KS):
+            weights = [
+                jnp.broadcast_to(taps[:, a * KS + shift_b : a * KS + shift_b + 1], (8, width))
+                for a in range(KS)
+            ]
+            for row in range(tile_rows + 2 * margin):
+                cells = window(main_ref[row, rows, :], edge_ref[row, rows, :], lane, shift_b - margin)
+                for shift_a in range(KS):
+                    if 0 <= row - shift_a < tile_rows:
+                        sums[row - shift_a] = sums[row - shift_a] + weights[shift_a] * cells
+        for row in range(tile_rows):
+            conv[rows, row * width : (row + 1) * width] = sums[row]
+        return carry
+
+    lax.fori_loop(0, eights, conv_step, 0)
+
+    gain = gain_ref[...]
+    block_rows = 2
+    block = block_rows * width
+
+    def cell_step(step, carry):
+        cells = pl.ds(pl.multiple_of(step * block, block), block)
+        conv_blk = conv[:, cells]
+        centred = conv_blk - jnp.mean(conv_blk, axis=0, keepdims=True)
+        inv_std = lax.rsqrt(jnp.mean(centred * centred, axis=0, keepdims=True) + norm_eps)
+        normed = centred * inv_std
+        scaled = (normed * gain).astype(jnp.bfloat16)
+        scaled_all[:, cells] = scaled
+        pre_act = jnp.dot(expand_t[...], scaled, preferred_element_type=jnp.float32)
+        normal_cdf = 0.5 * (1.0 + lax.erf(pre_act * root_half))
+        normal_pdf = jnp.exp(-0.5 * pre_act * pre_act) * gauss_norm
+        hidden = (pre_act * normal_cdf).astype(jnp.bfloat16)
+        gelu_slope = normal_cdf + pre_act * normal_pdf
+        d_hidden = jnp.dot(reduce_ref[...], cot_ref[:, cells], preferred_element_type=jnp.float32)
+        d_pre = (d_hidden * gelu_slope).astype(jnp.bfloat16)
+        hidden_all[:, cells] = hidden
+        d_pre_all[:, cells] = d_pre
+        branch = jnp.dot(reduce_t[...], hidden, preferred_element_type=jnp.float32)
+        for part in range(block_rows):
+            row = step * block_rows + part
+            at = pl.ds(pl.multiple_of(row * width, width), width)
+            total = main_ref[margin + row] + branch[:, part * width : (part + 1) * width]
+            state_out[:, at] = (total * mask_ref[:, at]).astype(jnp.bfloat16)
+        d_scaled = jnp.dot(expand_ref[...], d_pre, preferred_element_type=jnp.float32)
+        product = d_scaled * normed
+        for part in range(block_rows):
+            gain_sum[...] += product[:, part * width : (part + 1) * width]
+        d_normed = d_scaled * gain
+        mean_one = jnp.mean(d_normed, axis=0, keepdims=True)
+        mean_two = jnp.mean(d_normed * normed, axis=0, keepdims=True)
+        conv[:, cells] = inv_std * (d_normed - mean_one - normed * mean_two)
+        return carry
+
+    lax.fori_loop(0, tile_rows // block_rows, cell_step, 0)
+
+    over_cells = (((1,), (1,)), ((), ()))
+    for at, (low, high) in enumerate(spans):
+        grad = lax.dot_general(
+            scaled_all[...], d_pre_all[low:high, :], over_cells, preferred_element_type=jnp.float32
+        )
+        pack(big.acc, at * 2 * eights, 0, grad * scale)
+        grad = lax.dot_general(
+            cot_ref[...], hidden_all[low:high, :], over_cells, preferred_element_type=jnp.float32
+        )
+        pack(big.acc, at * 2 * eights, eights, grad * scale)
+
+    def depthwise_step(step, carry):
+        rows = pl.ds(pl.multiple_of(step * 8, 8), 8)
+        d_conv = [conv[rows, row * width : (row + 1) * width] for row in range(tile_rows)]
+        line = jnp.sum(gain_sum[rows, :], axis=1, keepdims=True)
+        line = jnp.where(lane == KS * KS, line, 0.0)
         for shift_b in range(KS):
-            window = padded[:, shift_a : shift_a + out_rows, shift_b : shift_b + out_cols].astype(
-                jnp.float32
-            )
-            columns.append(jnp.sum(d_conv * window, axis=(1, 2)))
-    return jnp.stack(columns, axis=1)
-
-
-def cell_pass(conv_blk, state_blk, cot_blk, mask_blk, norm_gain, expand_weight, reduce_weight):
-    chan_mean = jnp.mean(conv_blk, axis=0, keepdims=True)
-    centred = conv_blk - chan_mean
-    chan_var = jnp.mean(centred * centred, axis=0, keepdims=True)
-    inv_std = lax.rsqrt(chan_var + norm_eps)
-    normed = centred * inv_std
-    scaled = (normed * norm_gain[:, None]).astype(jnp.bfloat16)
-    pre_act = jnp.dot(expand_weight.T, scaled, preferred_element_type=jnp.float32)
-    normal_cdf = 0.5 * (1.0 + lax.erf(pre_act * root_half))
-    normal_pdf = jnp.exp(-0.5 * pre_act * pre_act) * gauss_norm
-    hidden = (pre_act * normal_cdf).astype(jnp.bfloat16)
-    gelu_slope = normal_cdf + pre_act * normal_pdf
-    branch = jnp.dot(reduce_weight.T, hidden, preferred_element_type=jnp.float32)
-    out_blk = ((state_blk.astype(jnp.float32) + branch) * mask_blk[None, :]).astype(jnp.bfloat16)
-    grad_reduce = jnp.dot(cot_blk, hidden.T, preferred_element_type=jnp.float32)
-    d_hidden = jnp.dot(reduce_weight, cot_blk, preferred_element_type=jnp.float32)
-    d_pre = (d_hidden * gelu_slope).astype(jnp.bfloat16)
-    grad_expand = jnp.dot(scaled, d_pre.T, preferred_element_type=jnp.float32)
-    d_scaled = jnp.dot(expand_weight, d_pre, preferred_element_type=jnp.float32)
-    grad_gain = jnp.sum(d_scaled * normed, axis=1)
-    d_normed = d_scaled * norm_gain[:, None]
-    d_conv = inv_std * (
-        d_normed
-        - jnp.mean(d_normed, axis=0, keepdims=True)
-        - normed * jnp.mean(d_normed * normed, axis=0, keepdims=True)
-    )
-    return (out_blk, d_conv, grad_expand, grad_reduce, grad_gain)
+            sums = [jnp.zeros((8, width), jnp.float32) for _ in range(KS)]
+            for row in range(tile_rows + 2 * margin):
+                cells = window(main_ref[row, rows, :], edge_ref[row, rows, :], lane, shift_b - margin)
+                for shift_a in range(KS):
+                    if 0 <= row - shift_a < tile_rows:
+                        sums[shift_a] = sums[shift_a] + d_conv[row - shift_a] * cells
+            for shift_a in range(KS):
+                total = jnp.sum(sums[shift_a], axis=1, keepdims=True)
+                line = jnp.where(lane == shift_a * KS + shift_b, total, line)
+        small.acc[pl.ds(step, 1)] = (line[:, :LANES] * scale).reshape(1, 8, LANES)
+        return carry
+
+    pl.semaphore_wait(barrier, barrier_count)
+    ahead, behind = big.steps(), small.steps()
+    next(ahead)
+    lax.fori_loop(0, eights // 2, depthwise_step, 0)
+    next(ahead)
+    lax.fori_loop(eights // 2, eights, depthwise_step, 0)
+    running = [behind, ahead]
+    while running:
+        running = [one for one in running if next(one, None) is not None]
+
+    for at, (low, high) in enumerate(spans):
+        both = big.full[at * eights : (at + 1) * eights].astype(jnp.float32)
+        both = both.reshape(2 * channels, LANES)
+        expand_out[:, low:high] = both[:channels, : high - low]
+        reduce_out[low:high, :] = both[channels:].T[: high - low, :]
+    rest = small.full[: -(-eights // 2)].astype(jnp.float32).reshape(-1, LANES)
+    small_out[...] = rest[:channels, : small_out.shape[1]]
+
+
+def block_call(sizes, scale, main, edge, cot, mask, dw_weight, norm_gain, expand_weight, reduce_weight):
+    channels, hidden = expand_weight.shape
+    cells = cot.shape[1]
+    eights = channels // 8
+    big = Reducer(sizes, big_streams(sizes), -(-hidden // LANES) * eights)
+    small = Reducer(sizes, small_streams(sizes), -(-eights // 2))
+    vmem = pl.BlockSpec(memory_space=pltpu.VMEM)
+    return pl.pallas_call(
+        functools.partial(block_kernel, big, small, scale),
+        out_shape=(
+            jax.ShapeDtypeStruct((channels, cells), jnp.bfloat16),
+            jax.ShapeDtypeStruct((channels, hidden), jnp.float32),
+            jax.ShapeDtypeStruct((hidden, channels), jnp.float32),
+            jax.ShapeDtypeStruct((channels, KS * KS + 1), jnp.float32),
+        ),
+        in_specs=[vmem] * 8,
+        out_specs=[vmem] * 4,
+        scratch_shapes=[
+            pltpu.VMEM((hidden, channels), jnp.bfloat16),
+            pltpu.VMEM((channels, hidden), jnp.bfloat16),
+            pltpu.VMEM((channels, cells), jnp.float32),
+            pltpu.VMEM((channels, cells), jnp.bfloat16),
+            pltpu.VMEM((hidden, cells), jnp.bfloat16),
+            pltpu.VMEM((hidden, cells), jnp.bfloat16),
+            pltpu.VMEM((channels, main.shape[2]), jnp.float32),
+        ]
+        + big.scratch()
+        + small.scratch(),
+        compiler_params=pltpu.CompilerParams(
+            collective_id=0, has_side_effects=True, vmem_limit_bytes=60 * 1024 * 1024
+        ),
+    )(main, edge, cot, mask, dw_weight, norm_gain[:, None], expand_weight, reduce_weight)
 
 
 def body(ocean_state, ocean_mask, dw_weight, norm_gain, expand_weight, reduce_weight, cotangent):
     state_tile = ocean_state[0]
-    channels = state_tile.shape[0]
-    tile_rows = state_tile.shape[1]
-    tile_cols = state_tile.shape[2]
+    channels, tile_rows, tile_cols = state_tile.shape
     margin = KS // 2
     mask_bf = ocean_mask.astype(jnp.bfloat16)
     masked = state_tile * mask_bf[None]
@@ -349,30 +454,34 @@
     padded = jnp.concatenate(
         [south_rows, padded[:, margin : tile_rows + margin, :], north_rows], axis=1
     )
-    conv_out = depthwise(padded, dw_weight, tile_rows, tile_cols)
+    padded = padded.transpose(1, 0, 2).astype(jnp.float32)
+    main = padded[:, :, margin : margin + tile_cols]
+    edge = jnp.concatenate(
+        [
+            padded[:, :, margin + tile_cols :],
+            jnp.zeros(main.shape[:2] + (tile_cols - 2 * margin,), jnp.float32),
+            padded[:, :, :margin],
+        ],
+        axis=2,
+    )
     cell_count = tile_rows * tile_cols
     cot_masked = (cotangent[0] * mask_bf[None]).reshape(channels, cell_count)
-    out_flat, d_conv, grad_expand, grad_reduce, grad_gain = cell_pass(
-        conv_out.reshape(channels, cell_count),
-        state_tile.reshape(channels, cell_count),
+    grad_scale = 1.0 / math.sqrt(lax.axis_size("ens") * lat_count * lon_count * cell_count)
+    sizes = {axis: lax.axis_size(axis) for axis in MESH_AXES}
+    out_flat, grad_expand, grad_reduce, small = block_call(
+        sizes,
+        grad_scale,
+        main,
+        edge,
         cot_masked,
-        ocean_mask.astype(jnp.float32).reshape(cell_count),
+        ocean_mask.astype(jnp.float32).reshape(1, cell_count),
+        dw_weight,
         norm_gain,
         expand_weight,
         reduce_weight,
     )
-    grad_depthwise = depthwise_grad(
-        d_conv.reshape(channels, tile_rows, tile_cols), padded, tile_rows, tile_cols
-    )
-    grad_scale = 1.0 / math.sqrt(lax.axis_size("ens") * lat_count * lon_count * cell_count)
-    sizes = {axis: lax.axis_size(axis) for axis in MESH_AXES}
-    small = jnp.concatenate([grad_depthwise, grad_gain[:, None]], axis=1)
-    grad_expand, grad_reduce, small = all_reduce(
-        sizes, grad_scale, grad_expand, grad_reduce, small
-    )
-    grad_depthwise, grad_gain = small[:, :-1], small[:, -1]
     next_state = out_flat.reshape(channels, tile_rows, tile_cols)[None]
-    return (next_state, grad_depthwise, grad_gain, grad_expand, grad_reduce)
+    return (next_state, small[:, :-1], small[:, -1], grad_expand, grad_reduce)
 
 
 def solution(mesh):

time: 139 us -> 98.8 us (0.71)
  local copies, waits for them, and re-layouts: 59.2 us -> 13.9 us
  Pallas kernels: 31 us -> 50 us
  other arithmetic: 23.2 us -> 5.72 us
  waiting for transfers between devices: 9.27 us -> 21.7 us
  matrix products: 9.15 us -> 0 us
  starting transfers between devices: 5.02 us -> 6.42 us
    another operation x49 -> x0, local copies, waits for them, and re-layouts: 38.7 us -> none  [depthwise_grad(): return jnp.stack(columns, axis=1)]
    reduce_sum x6 -> x0, other arithmetic: 21.2 us -> none  [the longest x4 12.6 us: depthwise_grad(): columns.append(jnp.sum(d_conv * window, axis=(1, 2)))]
    pallas_call x1, Pallas kernels: 31 us -> 50 us  [block_call(): pl.pallas_call(functools.partial(block_kernel, big, small, scale), out_sh...]
    dot_general x6 -> x0, matrix products: 9.15 us -> none  [the longest x1 2.18 us: cell_pass(): jnp.dot(expand_weight.T, scaled, preferred_element_type=jnp.float32)]
    concatenate x1, local copies, waits for them, and re-layouts: 5.77 us -> 0.08 us  [body(): jnp.concatenate([padded[:, :, margin + tile_cols:], jnp.zeros(main.shape[...]
    ppermute x2, waiting for transfers between devices: 2.02 us -> 7.66 us  [with_halo(): lax.ppermute(head, axis, [((i + 1) % count, i) for i in range(count)])]
    ppermute x2, waiting for transfers between devices: 3.92 us -> 8.16 us  [with_halo(): lax.ppermute(tail, axis, [(i, (i + 1) % count) for i in range(count)])]
    reshape x2 -> x0, local copies, waits for them, and re-layouts: 3.01 us -> none  [the longest x1 1.54 us: body(): conv_out.reshape(channels, cell_count)]
  transfers between devices with their start and end apart: 5 -> 5, of which waited for: 4 -> 4; matrix products, arithmetic and copies ran while one was open for 1% -> 5% of each run, Pallas kernels for 0% -> 0%
where the time goes in v2:
time: 98.8 us; the launch traced here: 98.6 us
  Pallas kernels  50 us (51%)
  waiting for transfers between devices  21.7 us (22%)
  local copies, waits for them, and re-layouts  13.9 us (14%)
  starting transfers between devices  6.42 us (6%)
  other arithmetic  5.72 us (6%)
    pallas_call x1, Pallas kernels, block_call(): pl.pallas_call(functools.partial(block_kernel, big, small, scale), out_sh...  50 us
    unnamed x20, local copies, waits for them, and re-layouts  9.23 us
    ppermute x2, waiting for transfers between devices, with_halo(): lax.ppermute(tail, axis, [(i, (i + 1) % count) for i in range(count)])  8.16 us
    ppermute x2, waiting for transfers between devices, with_halo(): lax.ppermute(head, axis, [((i + 1) % count, i) for i in range(count)])  7.66 us
    ppermute x1, waiting for transfers between devices, swapped(): lax.ppermute(array, axis, [(i, i ^ 1 << stride) for i in range(lax.axis_s...  5.91 us
    ppermute x2, starting transfers between devices, with_halo(): lax.ppermute(head, axis, [((i + 1) % count, i) for i in range(count)])  4.48 us
  transfers between devices with their start and end apart: 5, of which 4 were waited for; matrix products, arithmetic and copies ran while one was open for 5% of the time, Pallas kernels for 0%

profile of v2, /device:TPU:0, one launch (start us, length us, event | category | flops | bytes accessed | tf_op | source)
XLA Modules:
  0.0 98.6 jit_solution(8928363486198836451)
XLA Ops:
  0.7 1.4 %fusion.2 = (f32[8,128]{1,0:T(8,128)}, bf16[8,128]{1,0:T(8,128)(2,1)S(1)}) fusion(s32[8,128]{1,0:T(8,128)} %param.8), kind=kLoop, calls=%fused_computation.12 | loop fusion | flops 2048 | bytes 10240 | tf_op jit(solution)/shard_map/convert_element_type | solution.py:477
  2.0 1.1 %bitcast_multiply_fusion.1 = bf16[200,8,128]{2,0,1:T(8,128)(2,1)S(1)} fusion(bf16[1,200,8,128]{3,2,1,0:T(8,128)(2,1)} %param.7, bf16[8,128]{1,0:T(8,128)(2,1)S(1)} %get-tuple-element.30), kind=kLoop, calls=%fused_computation.3 | loop fusion | flops 204800 | bytes 821248 | tf_op jit(solution)/shard_map/mul | solution.py:443
  3.3 3.0 %collective-permute-start.1 = (bf16[200,8,3]{2,0,1:T(8,128)(2,1)S(1)}, bf16[200,8,3]{2,0,1:T(8,128)(2,1)S(1)}, u32[]{:S(2)}, u32[]{:S(2)}) collective-permute-start(bf16[200,8,3]{2,0,1:T(8,128)(2,1)S(1)} %get-tuple-element.28), channel_id=1, source_target_pairs={{4,0},{0,4},{5,1},{1,5},{6,2},{2,6},{7,3},{3,7},{12,8},{8,12},{13,... | collective-permute-start | bytes 28808 | tf_op jit(solution)/shard_map/ppermute | solution.py:224
  6.4 0.7 copy.18.dw_ref
  7.1 0.8 copy.19.gain_ref
  7.9 0.9 copy.20.reduce_ref
  8.9 7.7 %collective-permute-done.1 = bf16[200,8,3]{2,0,1:T(8,128)(2,1)S(1)} collective-permute-done((bf16[200,8,3]{2,0,1:T(8,128)(2,1)S(1)}, bf16[200,8,3]{2,0,1:T(8,128)(2,1)S(1)}, u32[]{:S(2)}, u32[]{:S(2)}) %collective-permute-start.1) | collective-permute-done | bytes 9632 | tf_op jit(solution)/shard_map/ppermute | solution.py:224
  16.6 7.9 %collective-permute-done = bf16[200,8,3]{2,0,1:T(8,128)(2,1)S(1)} collective-permute-done((bf16[200,8,3]{2,0,1:T(8,128)(2,1)S(1)}, bf16[200,8,3]{2,0,1:T(8,128)(2,1)S(1)}, u32[]{:S(2)}, u32[]{:S(2)}) %collective-permute-start) | collective-permute-done | bytes 9632 | tf_op jit(solution)/shard_map/ppermute | solution.py:222
  24.5 0.4 pad_maximum_fusion.1
  25.0 0.8 bitcast_multiply_fusion.cot_ref
  25.8 1.8 %reverse = bf16[200,3,256]{2,0,1:T(8,128)(2,1)S(1)} reverse(bf16[200,3,256]{2,0,1:T(8,128)(2,1)S(1)} %bitcast.16), dimensions={1,2} | reverse | bytes 614400
  27.8 1.8 %collective-permute-start.3 = (bf16[200,3,134]{2,0,1:T(8,128)(2,1)S(1)}, bf16[200,3,134]{2,0,1:T(8,128)(2,1)S(1)}, u32[]{:S(2)}, u32[]{:S(2)}) collective-permute-start(bf16[200,3,134]{2,0,1:T(8,128)(2,1)S(1)} %slice.43), channel_id=1, source_target_pairs={{0,4},{4,0},{1,5},{5,1},{2,6},{6,2},{3,7},{7,3},{8,12},{12,8},{9,1... | collective-permute-start | bytes 482408 | tf_op jit(solution)/shard_map/ppermute | solution.py:232
  29.6 1.4 %collective-permute-start.4 = (bf16[200,3,134]{2,0,1:T(8,128)(2,1)S(1)}, bf16[200,3,134]{2,0,1:T(8,128)(2,1)S(1)}, u32[]{:S(2)}, u32[]{:S(2)}) collective-permute-start(bf16[200,3,134]{2,0,1:T(8,128)(2,1)S(1)} %get-tuple-element.25), channel_id=1, source_target_pairs={{1,0},{2,1},{3,2},{0,3},{5,4},{6,5},{7,6},{4,7},{9,8},{10,9},{11,1... | collective-permute-start | bytes 482408 | tf_op jit(solution)/shard_map/ppermute | solution.py:224
  31.3 5.9 %collective-permute-done.3 = bf16[200,3,134]{2,0,1:T(8,128)(2,1)S(1)} collective-permute-done((bf16[200,3,134]{2,0,1:T(8,128)(2,1)S(1)}, bf16[200,3,134]{2,0,1:T(8,128)(2,1)S(1)}, u32[]{:S(2)}, u32[]{:S(2)}) %collective-permute-start.3) | collective-permute-done | bytes 160832 | tf_op jit(solution)/shard_map/ppermute | solution.py:232
  37.2 0.5 convert_bitcast_fusion
  37.7 1.6 %slice.39.main_ref = f32[14,200,128]{2,1,0:T(8,128)} slice(f32[14,200,134]{2,1,0:T(8,128)S(1)} %convert_bitcast_fusion), slice={[0:14], [0:200], [3:131]} | slice | bytes 2867200 | tf_op jit(solution)/shard_map/slice | solution.py:458
  39.3 0.4 fusion
  39.7 1.6 %pad_maximum_fusion.edge_ref = f32[14,200,128]{2,1,0:T(8,128)} fusion(f32[14,200,3]{2,1,0:T(8,128)S(1)} %get-tuple-element.24, f32[14,200,3]{2,1,0:T(8,128)S(1)} %get-tuple-element.23, f32[128]{0:T(128)S(1)} %pad.1.clone), kind=kLoop, calls=%fused_computation.1 | loop fusion | flops 716800 | bytes 1501312 | tf_op jit(solution)/shard_map/concatenate | solution.py:459
  41.3 50.0 %shard_map.110 = (bf16[200,1024]{1,0:T(8,128)(2,1)}, f32[200,800]{1,0:T(8,128)}, f32[800,200]{1,0:T(8,128)}, f32[200,50]{1,0:T(8,128)}) custom-call(f32[14,200,128]{2,1,0:T(8,128)} %slice.39.main_ref, f32[14,200,128]{2,1,0:T(8,128)} %pad_maximum_fusion.edge_ref, bf16[200,1024]{1,0:T(8,128)(2,1)} %bitcast_multiply_fusion.cot_ref, f32[1,1024]{1,0:T(1,128)} %bitcast.22, ...), custom_call_target="tpu_custom_call" | custom-call | tf_op jit(solution)/shard_map/pallas_call | solution.py:411
  91.4 1.9 %copy.24 = bf16[25,8,8,128]{3,2,1,0:T(8,128)(2,1)} copy(bf16[25,8,8,128]{3,1,2,0:T(8,128)(2,1)} %bitcast.19) | data formatting | bytes 819200
  93.3 1.6 %slice_reduce_fusion = f32[200]{0:T(256)} fusion(f32[200,50]{1,0:T(8,128)} %get-tuple-element.10), kind=kLoop, calls=%fused_computation.9 | loop fusion | bytes 1600 | tf_op jit(solution)/shard_map/slice | solution.py:484
  95.0 1.6 %copy.21 = f32[200,49]{0,1:T(8,128)} copy(f32[200,49]{1,0:T(8,128)} %bitcast.20) | data formatting | bytes 78400
  96.6 1.1 %copy.22 = f32[800,200]{0,1:T(8,128)} copy(f32[800,200]{1,0:T(8,128)S(1)} %copy-done) | data formatting | bytes 1280000
  97.7 0.9 copy.28
  (22 shorter events, 0.8 us)
Async XLA Ops:
  0.6 5.7 %copy-start.4 = (f32[200,49]{0,1:T(8,128)S(1)}, f32[200,49]{0,1:T(8,128)}, u32[]{:S(2)}) copy-start(f32[200,49]{0,1:T(8,128)} %param.9) | copy-start | bytes 117604
  0.6 6.5 %copy-start.5 = (f32[200]{0:T(256)S(1)}, f32[200]{0:T(256)}, u32[]{:S(2)}) copy-start(f32[200]{0:T(256)} %param.10) | copy-start | bytes 2404
  0.7 7.3 %copy-start.3 = (bf16[800,200]{0,1:T(8,128)(2,1)S(1)}, bf16[800,200]{0,1:T(8,128)(2,1)}, u32[]{:S(2)}) copy-start(bf16[800,200]{0,1:T(8,128)(2,1)} %param.12) | copy-start | bytes 960004
  3.3 13.3 %collective-permute-start.1 = (bf16[200,8,3]{2,0,1:T(8,128)(2,1)S(1)}, bf16[200,8,3]{2,0,1:T(8,128)(2,1)S(1)}, u32[]{:S(2)}, u32[]{:S(2)}) collective-permute-start(bf16[200,8,3]{2,0,1:T(8,128)(2,1)S(1)} %get-tuple-element.28), channel_id=1, source_target_pairs={{4,0},{0,4},{5,1},{1,5},{6,2},{2,6},{7,3},{3,7},{12,8},{8,12},{13,... | collective-permute-start | bytes 28808 | tf_op jit(solution)/shard_map/ppermute | solution.py:224
  6.3 18.2 %collective-permute-start = (bf16[200,8,3]{2,0,1:T(8,128)(2,1)S(1)}, bf16[200,8,3]{2,0,1:T(8,128)(2,1)S(1)}, u32[]{:S(2)}, u32[]{:S(2)}) collective-permute-start(bf16[200,8,3]{2,0,1:T(8,128)(2,1)S(1)} %get-tuple-element.27), channel_id=1, source_target_pairs={{0,4},{4,0},{1,5},{5,1},{2,6},{6,2},{3,7},{7,3},{8,12},{12,8},{9,1... | collective-permute-start | bytes 28808 | tf_op jit(solution)/shard_map/ppermute | solution.py:222
  6.4 18.6 %copy-start.2 = (bf16[1,200,8,128]{3,2,1,0:T(8,128)(2,1)S(1)}, bf16[1,200,8,128]{3,2,1,0:T(8,128)(2,1)}, u32[]{:S(2)}) copy-start(bf16[1,200,8,128]{3,2,1,0:T(8,128)(2,1)} %param.13) | copy-start | bytes 1228804
  24.9 6.3 %collective-permute-start.2 = (bf16[200,3,134]{2,0,1:T(8,128)(2,1)S(1)}, bf16[200,3,134]{2,0,1:T(8,128)(2,1)S(1)}, u32[]{:S(2)}, u32[]{:S(2)}) collective-permute-start(bf16[200,3,134]{2,0,1:T(8,128)(2,1)S(1)} %get-tuple-element.26), channel_id=1, source_target_pairs={{0,1},{1,2},{2,3},{3,0},{4,5},{5,6},{6,7},{7,4},{8,9},{9,10},{10,1... | collective-permute-start | bytes 482408 | tf_op jit(solution)/shard_map/ppermute | solution.py:222
  27.8 9.4 %collective-permute-start.3 = (bf16[200,3,134]{2,0,1:T(8,128)(2,1)S(1)}, bf16[200,3,134]{2,0,1:T(8,128)(2,1)S(1)}, u32[]{:S(2)}, u32[]{:S(2)}) collective-permute-start(bf16[200,3,134]{2,0,1:T(8,128)(2,1)S(1)} %slice.43), channel_id=1, source_target_pairs={{0,4},{4,0},{1,5},{5,1},{2,6},{6,2},{3,7},{7,3},{8,12},{12,8},{9,1... | collective-permute-start | bytes 482408 | tf_op jit(solution)/shard_map/ppermute | solution.py:232
  29.6 7.6 %collective-permute-start.4 = (bf16[200,3,134]{2,0,1:T(8,128)(2,1)S(1)}, bf16[200,3,134]{2,0,1:T(8,128)(2,1)S(1)}, u32[]{:S(2)}, u32[]{:S(2)}) collective-permute-start(bf16[200,3,134]{2,0,1:T(8,128)(2,1)S(1)} %get-tuple-element.25), channel_id=1, source_target_pairs={{1,0},{2,1},{3,2},{0,3},{5,4},{6,5},{7,6},{4,7},{9,8},{10,9},{11,1... | collective-permute-start | bytes 482408 | tf_op jit(solution)/shard_map/ppermute | solution.py:224
  91.4 5.2 %copy-start = (f32[800,200]{1,0:T(8,128)S(1)}, f32[800,200]{1,0:T(8,128)}, u32[]{:S(2)}) copy-start(f32[800,200]{1,0:T(8,128)} %get-tuple-element.22) | copy-start | bytes 1920004
  91.4 6.4 %copy-start.1 = (f32[200,800]{1,0:T(8,128)S(1)}, f32[200,800]{1,0:T(8,128)}, u32[]{:S(2)}) copy-start(f32[200,800]{1,0:T(8,128)} %get-tuple-element.39) | copy-start | bytes 1920004

commit v3 on v2

--- a/solution.py
+++ b/solution.py
@@ -212,26 +212,6 @@
     acc[begin : begin + rows // 8, :, :width] = block.reshape(rows // 8, 8, width)
 
 
-def with_halo(cells, sides, width):
-    for axis, dim in sides:
-        count = lax.axis_size(axis)
-        head = lax.slice_in_dim(cells, 0, width, axis=dim)
-        tail = lax.slice_in_dim(cells, cells.shape[dim] - width, cells.shape[dim], axis=dim)
-        cells = jnp.concatenate(
-            [
-                lax.ppermute(tail, axis, [(i, (i + 1) % count) for i in range(count)]),
-                cells,
-                lax.ppermute(head, axis, [((i + 1) % count, i) for i in range(count)]),
-            ],
-            axis=dim,
-        )
-    return cells
-
-
-def swapped(array, axis, stride):
-    return lax.ppermute(array, axis, [(i, i ^ 1 << stride) for i in range(lax.axis_size(axis))])
-
-
 def lane_spans(width):
     return [(low, min(low + LANES, width)) for low in range(0, width, LANES)]
 
@@ -244,12 +224,174 @@
     return pltpu.roll(jnp.where(outside, edge, main), (-shift) % width, 1)
 
 
+class Halo:
+    def __init__(self, sizes, margin, rows, channels, width):
+        self.sizes, self.margin, self.rows = sizes, margin, rows
+        self.channels, self.width = channels, width
+        self.pitch = width // rows
+
+    def scratch(self):
+        packed = (self.channels, self.width)
+        return [
+            pltpu.VMEM(packed, jnp.bfloat16),
+            pltpu.VMEM((2,) + packed, jnp.bfloat16),
+            pltpu.VMEM(packed, jnp.bfloat16),
+            pltpu.VMEM((2,) + packed, jnp.bfloat16),
+            pltpu.VMEM((2, self.margin) + packed, jnp.bfloat16),
+            pltpu.SemaphoreType.DMA((2,)),
+            pltpu.SemaphoreType.DMA((2,)),
+            pltpu.SemaphoreType.DMA((2,)),
+            pltpu.SemaphoreType.DMA((2,)),
+            pltpu.SemaphoreType.DMA((2,)),
+            pltpu.SemaphoreType.DMA((2,)),
+        ]
+
+    def bind(self, cells, main, edge, pack_out, pack_in, corner_out, corner_in, strip_in, *sems):
+        self.cells, self.main, self.edge = cells, main, edge
+        self.pack_out, self.pack_in = pack_out, pack_in
+        self.corner_out, self.corner_in, self.strip_in = corner_out, corner_in, strip_in
+        lon, lat = lax.axis_index("lon"), lax.axis_index("lat")
+        lons, lats = self.sizes["lon"], self.sizes["lat"]
+        self.south_open = lat > 0
+        self.top = lat == lats - 1
+        mirror = lons - 1 - lon
+        self.left = {"lon": lax.rem(lon + lons - 1, lons)}
+        self.right = {"lon": lax.rem(lon + 1, lons)}
+        self.peers = [self.left, self.right, {"lon": mirror}]
+        up = {
+            "lon": jnp.where(self.top, mirror, lon),
+            "lat": jnp.where(self.top, lat, lat + 1),
+        }
+        down = {"lat": jnp.where(self.south_open, lat - 1, lat + 1)}
+        slot = jnp.where(self.top, 1, 0)
+        lon_send, lon_recv, strip_send, strip_recv, corner_send, corner_recv = sems
+        self.lon_copies = [
+            self.copy(pack_out, pack_in.at[0], lon_send.at[0], lon_recv.at[0], self.left)
+        ]
+        if lons > 2:
+            self.lon_copies.append(
+                self.copy(pack_out, pack_in.at[1], lon_send.at[1], lon_recv.at[1], self.right)
+            )
+        high = cells.at[pl.ds(self.rows - self.margin, self.margin)]
+        low = cells.at[pl.ds(0, self.margin)]
+        self.up_strip = self.copy(high, strip_in.at[slot], strip_send.at[0], strip_recv.at[slot], up)
+        self.down_strip = self.copy(low, strip_in.at[1], strip_send.at[1], strip_recv.at[1], down)
+        self.up_corner = self.copy(
+            corner_out, corner_in.at[slot], corner_send.at[0], corner_recv.at[slot], up
+        )
+        self.down_corner = self.copy(
+            corner_out, corner_in.at[1], corner_send.at[1], corner_recv.at[1], down
+        )
+        self.arrivals = [
+            [
+                self.copy(low, strip_in.at[side], strip_send.at[0], strip_recv.at[side], up),
+                self.copy(corner_out, corner_in.at[side], corner_send.at[0], corner_recv.at[side], up),
+            ]
+            for side in range(2)
+        ]
+        self.lane = lax.broadcasted_iota(jnp.int32, (self.channels, self.width), 1)
+
+    def copy(self, src, dst, send_sem, recv_sem, device):
+        return pltpu.make_async_remote_copy(
+            src_ref=src,
+            dst_ref=dst,
+            send_sem=send_sem,
+            recv_sem=recv_sem,
+            device_id=device,
+            device_id_type=pl.DeviceIdType.MESH,
+        )
+
+    def pack_columns(self):
+        packed = jnp.zeros((self.channels, self.width), jnp.float32)
+        for row in range(self.rows):
+            turned = pltpu.roll(
+                self.cells[row].astype(jnp.float32), row * self.pitch + self.margin, 1
+            )
+            packed = jnp.where(self.lane >= row * self.pitch, turned, packed)
+        self.pack_out[...] = packed.astype(jnp.bfloat16)
+
+    def unpacked(self, packed, row):
+        shift = (self.width - row * self.pitch - self.margin) % self.width
+        return pltpu.roll(packed, shift, 1)
+
+    def start(self):
+        for copy in self.lon_copies:
+            copy.start()
+        self.up_strip.start()
+        pl.when(self.south_open)(self.down_strip.start)
+
+    def spread_rows(self):
+        for row in range(self.rows):
+            self.main[self.margin + row] = self.cells[row].astype(jnp.float32)
+
+    def forward_corners(self):
+        for copy in self.lon_copies:
+            copy.wait_recv()
+        packed = self.pack_in[0].astype(jnp.float32)
+        if len(self.lon_copies) > 1:
+            from_left = self.pack_in[1].astype(jnp.float32)
+            packed = jnp.where(lax.rem(self.lane, self.pitch) < self.margin, from_left, packed)
+        self.corner_out[...] = packed.astype(jnp.bfloat16)
+        self.up_corner.start()
+        pl.when(self.south_open)(self.down_corner.start)
+        for row in range(self.rows):
+            self.edge[self.margin + row] = self.unpacked(packed, row)
+
+    def finish(self):
+        margin, rows = self.margin, self.rows
+
+        @pl.when(self.south_open)
+        def _():
+            for copy in self.arrivals[0]:
+                copy.wait_recv()
+            packed = self.corner_in[0].astype(jnp.float32)
+            for at in range(margin):
+                self.main[at] = self.strip_in[0, at].astype(jnp.float32)
+                self.edge[at] = self.unpacked(packed, rows - margin + at)
+
+        @pl.when(jnp.logical_not(self.south_open))
+        def _():
+            for at in range(margin):
+                self.main[at] = jnp.zeros((self.channels, self.width), jnp.float32)
+                self.edge[at] = jnp.zeros((self.channels, self.width), jnp.float32)
+
+        for copy in self.arrivals[1]:
+            copy.wait_recv()
+        north = margin + rows
+
+        @pl.when(self.top)
+        def _():
+            one = lax.broadcasted_iota(jnp.int32, (self.width, self.width), 0)
+            two = lax.broadcasted_iota(jnp.int32, (self.width, self.width), 1)
+            turn = jnp.where(one + two == self.width - 1, 1.0, 0.0).astype(jnp.bfloat16)
+            packed = self.corner_in[1].astype(jnp.float32)
+            for at in range(margin):
+                self.main[north + at] = jnp.dot(
+                    self.strip_in[1, margin - 1 - at], turn, preferred_element_type=jnp.float32
+                )
+                sides = self.unpacked(packed, rows - 1 - at).astype(jnp.bfloat16)
+                self.edge[north + at] = jnp.dot(sides, turn, preferred_element_type=jnp.float32)
+
+        @pl.when(jnp.logical_not(self.top))
+        def _():
+            packed = self.corner_in[1].astype(jnp.float32)
+            for at in range(margin):
+                self.main[north + at] = self.strip_in[1, at].astype(jnp.float32)
+                self.edge[north + at] = self.unpacked(packed, at)
+
+    def drain(self):
+        for copy in self.lon_copies + [self.up_strip, self.up_corner]:
+            copy.wait_send()
+        pl.when(self.south_open)(self.down_strip.wait_send)
+        pl.when(self.south_open)(self.down_corner.wait_send)
+
+
 def block_kernel(
     big,
     small,
+    halo,
     scale,
-    main_ref,
-    edge_ref,
+    cells_ref,
     cot_ref,
     mask_ref,
     dw_ref,
@@ -259,7 +401,10 @@
     state_out,
     expand_out,
     reduce_out,
-    small_out,
+    taps_out,
+    gain_out,
+    main_ref,
+    edge_ref,
     expand_t,
     reduce_t,
     conv,
@@ -276,14 +421,18 @@
     width = main_ref.shape[2]
     spans = lane_spans(hidden_units)
     big.bind(*scratch[:8])
-    small.bind(*scratch[8:])
-    peers = big.peers() + small.peers()
+    small.bind(*scratch[8:16])
+    halo.bind(cells_ref, main_ref, edge_ref, *scratch[16:])
+    peers = big.peers() + small.peers() + halo.peers
     barrier_count = len(peers)
     barrier = pltpu.get_barrier_semaphore()
     for device in peers:
         pl.semaphore_signal(
             barrier, inc=1, device_id=device, device_id_type=pl.DeviceIdType.MESH
         )
+    halo.pack_columns()
+    pl.semaphore_wait(barrier, barrier_count)
+    halo.start()
     big.clear()
     small.clear()
     gain_sum[...] = jnp.zeros_like(gain_sum)
@@ -292,6 +441,9 @@
         expand_t[low:high, :] = piece.astype(jnp.bfloat16)
         piece = reduce_ref[low:high, :].astype(jnp.float32).T
         reduce_t[:, low:high] = piece.astype(jnp.bfloat16)
+    halo.spread_rows()
+    halo.forward_corners()
+    halo.finish()
     lane = lax.broadcasted_iota(jnp.int32, (8, width), 1)
 
     def conv_step(step, carry):
@@ -382,7 +534,6 @@
         small.acc[pl.ds(step, 1)] = (line[:, :LANES] * scale).reshape(1, 8, LANES)
         return carry
 
-    pl.semaphore_wait(barrier, barrier_count)
     ahead, behind = big.steps(), small.steps()
     next(ahead)
     lax.fori_loop(0, eights // 2, depthwise_step, 0)
@@ -398,81 +549,65 @@
         expand_out[:, low:high] = both[:channels, : high - low]
         reduce_out[low:high, :] = both[channels:].T[: high - low, :]
     rest = small.full[: -(-eights // 2)].astype(jnp.float32).reshape(-1, LANES)
-    small_out[...] = rest[:channels, : small_out.shape[1]]
-
-
-def block_call(sizes, scale, main, edge, cot, mask, dw_weight, norm_gain, expand_weight, reduce_weight):
+    taps_out[...] = rest[:channels, : KS * KS]
+    gain_out[...] = rest[:channels, KS * KS : KS * KS + 1]
+    halo.drain()
+
+
+def block_call(sizes, scale, masked, cot, mask, dw_weight, norm_gain, expand_weight, reduce_weight):
     channels, hidden = expand_weight.shape
     cells = cot.shape[1]
     eights = channels // 8
     big = Reducer(sizes, big_streams(sizes), -(-hidden // LANES) * eights)
     small = Reducer(sizes, small_streams(sizes), -(-eights // 2))
+    rows, _, width = masked.shape
+    halo = Halo(sizes, KS // 2, rows, channels, width)
+    padded = pltpu.VMEM((rows + 2 * (KS // 2), channels, width), jnp.float32)
     vmem = pl.BlockSpec(memory_space=pltpu.VMEM)
     return pl.pallas_call(
-        functools.partial(block_kernel, big, small, scale),
+        functools.partial(block_kernel, big, small, halo, scale),
         out_shape=(
             jax.ShapeDtypeStruct((channels, cells), jnp.bfloat16),
             jax.ShapeDtypeStruct((channels, hidden), jnp.float32),
             jax.ShapeDtypeStruct((hidden, channels), jnp.float32),
-            jax.ShapeDtypeStruct((channels, KS * KS + 1), jnp.float32),
+            jax.ShapeDtypeStruct((channels, KS * KS), jnp.float32),
+            jax.ShapeDtypeStruct((channels, 1), jnp.float32),
         ),
-        in_specs=[vmem] * 8,
-        out_specs=[vmem] * 4,
+        in_specs=[vmem] * 7,
+        out_specs=[vmem] * 5,
         scratch_shapes=[
+            padded,
+            padded,
             pltpu.VMEM((hidden, channels), jnp.bfloat16),
             pltpu.VMEM((channels, hidden), jnp.bfloat16),
             pltpu.VMEM((channels, cells), jnp.float32),
             pltpu.VMEM((channels, cells), jnp.bfloat16),
             pltpu.VMEM((hidden, cells), jnp.bfloat16),
             pltpu.VMEM((hidden, cells), jnp.bfloat16),
-            pltpu.VMEM((channels, main.shape[2]), jnp.float32),
+            pltpu.VMEM((channels, width), jnp.float32),
         ]
         + big.scratch()
-        + small.scratch(),
+        + small.scratch()
+        + halo.scratch(),
         compiler_params=pltpu.CompilerParams(
             collective_id=0, has_side_effects=True, vmem_limit_bytes=60 * 1024 * 1024
         ),
-    )(main, edge, cot, mask, dw_weight, norm_gain[:, None], expand_weight, reduce_weight)
+    )(masked, cot, mask, dw_weight, norm_gain[:, None], expand_weight, reduce_weight)
 
 
 def body(ocean_state, ocean_mask, dw_weight, norm_gain, expand_weight, reduce_weight, cotangent):
     state_tile = ocean_state[0]
     channels, tile_rows, tile_cols = state_tile.shape
-    margin = KS // 2
     mask_bf = ocean_mask.astype(jnp.bfloat16)
-    masked = state_tile * mask_bf[None]
-    padded = with_halo(masked, (("lon", 2), ("lat", 1)), margin)
-    lat_now = lax.axis_index("lat")
-    lat_count = lax.axis_size("lat")
-    lon_count = lax.axis_size("lon")
-    top_strip = padded[:, tile_rows : tile_rows + margin, :][:, ::-1, ::-1]
-    mirrored = top_strip
-    for bit_number in range(lon_count.bit_length() - 1):
-        mirrored = swapped(mirrored, "lon", bit_number)
-    north_rows = jnp.where(lat_now == lat_count - 1, mirrored, padded[:, tile_rows + margin :, :])
-    south_rows = jnp.where(lat_now == 0, jnp.zeros_like(top_strip), padded[:, :margin, :])
-    padded = jnp.concatenate(
-        [south_rows, padded[:, margin : tile_rows + margin, :], north_rows], axis=1
-    )
-    padded = padded.transpose(1, 0, 2).astype(jnp.float32)
-    main = padded[:, :, margin : margin + tile_cols]
-    edge = jnp.concatenate(
-        [
-            padded[:, :, margin + tile_cols :],
-            jnp.zeros(main.shape[:2] + (tile_cols - 2 * margin,), jnp.float32),
-            padded[:, :, :margin],
-        ],
-        axis=2,
-    )
+    masked = (state_tile * mask_bf[None]).transpose(1, 0, 2)
     cell_count = tile_rows * tile_cols
     cot_masked = (cotangent[0] * mask_bf[None]).reshape(channels, cell_count)
-    grad_scale = 1.0 / math.sqrt(lax.axis_size("ens") * lat_count * lon_count * cell_count)
     sizes = {axis: lax.axis_size(axis) for axis in MESH_AXES}
-    out_flat, grad_expand, grad_reduce, small = block_call(
+    grad_scale = 1.0 / math.sqrt(math.prod(sizes.values()) * cell_count)
+    out_flat, grad_expand, grad_reduce, taps, gain = block_call(
         sizes,
         grad_scale,
-        main,
-        edge,
+        masked,
         cot_masked,
         ocean_mask.astype(jnp.float32).reshape(1, cell_count),
         dw_weight,
@@ -481,7 +616,7 @@
         reduce_weight,
     )
     next_state = out_flat.reshape(channels, tile_rows, tile_cols)[None]
-    return (next_state, small[:, :-1], small[:, -1], grad_expand, grad_reduce)
+    return (next_state, taps, gain[:, 0], grad_expand, grad_reduce)
 
 
 def solution(mesh):

time: 98.8 us -> 72.6 us (0.73)
  waiting for transfers between devices: 21.7 us -> 0 us
  Pallas kernels: 50 us -> 57.8 us
  starting transfers between devices: 6.42 us -> 0 us
  local copies, waits for them, and re-layouts: 13.9 us -> 8.15 us
    ppermute x5 -> x0, waiting for transfers between devices: 21.7 us -> none  [the longest x2 8.16 us: with_halo(): lax.ppermute(tail, axis, [(i, (i + 1) % count) for i in range(count)])]
    pallas_call x1, Pallas kernels: 50 us -> 57.8 us  [block_call(): pl.pallas_call(functools.partial(block_kernel, big, small, halo, scale),...]
    ppermute x5 -> x0, starting transfers between devices: 6.42 us -> none  [the longest x2 4.48 us: with_halo(): lax.ppermute(head, axis, [((i + 1) % count, i) for i in range(count)])]
    slice x4 -> x0, local copies, waits for them, and re-layouts: 3.82 us -> none  [the longest x1 1.64 us: body(): return (next_state, small[:, :-1], small[:, -1], grad_expand, grad_reduce)]
    concatenate x2 -> x0, other arithmetic: 1.93 us -> none  [the longest x1 1.56 us: body(): jnp.concatenate([padded[:, :, margin + tile_cols:], jnp.zeros(main.shape[...]
    unnamed x20 -> x18, local copies, waits for them, and re-layouts: 9.23 us -> 7.39 us
    pallas_call x0 -> x1, other arithmetic: none -> 1.6 us  [block_call(): pl.pallas_call(functools.partial(block_kernel, big, small, halo, scale),...]
    mul x1 -> x0, other arithmetic: 1.06 us -> none  [body(): masked = state_tile * mask_bf[None]]
  transfers between devices with their start and end apart: 5 -> 0, of which waited for: 4 -> 0; matrix products, arithmetic and copies ran while one was open for 5% -> 0% of each run, Pallas kernels for 0% -> 0%
where the time goes in v3:
time: 72.6 us; the launch traced here: 72.3 us
  Pallas kernels  57.8 us (80%)
  local copies, waits for them, and re-layouts  8.15 us (11%)
  other arithmetic  5.63 us (8%)
    pallas_call x1, Pallas kernels, block_call(): pl.pallas_call(functools.partial(block_kernel, big, small, halo, scale),...  57.8 us
    unnamed x18, local copies, waits for them, and re-layouts  7.39 us
    mul x1, other arithmetic, body(): cot_masked = (cotangent[0] * mask_bf[None]).reshape(channels, cell_count)  1.86 us
    pallas_call x1, other arithmetic, block_call(): pl.pallas_call(functools.partial(block_kernel, big, small, halo, scale),...  1.6 us

profile of v3, /device:TPU:0, one launch (start us, length us, event | category | flops | bytes accessed | tf_op | source)
XLA Modules:
  0.0 72.3 jit_solution(13562790773443497925)
XLA Ops:
  0.6 1.4 %fusion.1 = (f32[8,128]{1,0:T(8,128)}, bf16[8,128]{1,0:T(8,128)(2,1)S(1)}) fusion(s32[8,128]{1,0:T(8,128)} %param.8), kind=kLoop, calls=%fused_computation.3 | loop fusion | flops 2048 | bytes 10240 | tf_op jit(solution)/shard_map/convert_element_type | solution.py:612
  2.0 0.0 copy-start.5
  2.0 1.6 %copy.18.dw_ref = f32[200,49]{1,0:T(8,128)} copy(f32[200,49]{0,1:T(8,128)} %param.9) | data formatting | bytes 78400 | tf_op args[2]
  3.6 0.0 copy-done.5
  3.6 0.8 %copy.19.gain_ref = f32[200,1]{1,0:T(8,128)} copy(f32[200,1]{0,1:T(1,128)S(1)} %bitcast.21) | data formatting | bytes 1600 | tf_op jit(solution)/shard_map/broadcast_in_dim | solution.py:595
  4.3 0.0 copy-start.2
  4.3 1.9 %bitcast_multiply_fusion.cot_ref = bf16[200,1024]{1,0:T(8,128)(2,1)} fusion(bf16[25,8,8,128]{3,2,1,0:T(8,128)(2,1)} %bitcast.16, bf16[1024]{0:T(1024)(128)(2,1)S(1)} %bitcast.19), kind=kLoop, calls=%fused_computation | loop fusion | flops 204800 | bytes 821248 | tf_op jit(solution)/shard_map/mul | solution.py:604
  6.2 0.0 copy-done.2
  6.2 0.0 copy-start.3
  6.2 0.8 %fusion.cells_ref = bf16[8,200,128]{2,1,0:T(8,128)(2,1)} fusion(bf16[1,200,8,128]{3,2,1,0:T(8,128)(2,1)S(1)} %copy-done.2, bf16[8,128]{1,0:T(8,128)(2,1)S(1)} %get-tuple-element.26), kind=kLoop, calls=%fused_computation.2 | loop fusion | flops 204800 | bytes 821248 | tf_op jit(solution)/shard_map/transpose | solution.py:602
  7.0 0.2 copy-done.3
  7.2 0.9 %copy.20.reduce_ref = bf16[800,200]{1,0:T(8,128)(2,1)} copy(bf16[800,200]{0,1:T(8,128)(2,1)S(1)} %copy-done.3) | data formatting | bytes 640000 | tf_op args[5]
  8.2 57.8 %shard_map.110 = (bf16[200,1024]{1,0:T(8,128)(2,1)}, f32[200,800]{1,0:T(8,128)}, f32[800,200]{1,0:T(8,128)}, f32[200,49]{1,0:T(8,128)}, f32[200,1]{1,0:T(8,128)}) custom-call(bf16[8,200,128]{2,1,0:T(8,128)(2,1)} %fusion.cells_ref, bf16[200,1024]{1,0:T(8,128)(2,1)} %bitcast_multiply_fusion.cot_ref, f32[1,1024]{1,0:T(1,128)} %bitcast.20, ...), custom_call_target="tpu_custom_call" | custom-call | tf_op jit(solution)/shard_map/pallas_call | solution.py:567
  66.0 0.0 copy-start
  66.1 1.9 %copy.24 = bf16[25,8,8,128]{3,2,1,0:T(8,128)(2,1)} copy(bf16[25,8,8,128]{3,1,2,0:T(8,128)(2,1)} %bitcast.18) | data formatting | bytes 819200
  68.0 0.0 copy-start.4
  68.0 1.6 %reduce = f32[200]{0:T(256)} reduce(f32[200,1]{1,0:T(8,128)} %get-tuple-element.12, f32[]{:T(128)} %constant.2), dimensions={1}, to_apply=%get-tuple-element.12.reduce_sub_computation | reduce | bytes 1604 | tf_op jit(solution)/shard_map/pallas_call | solution.py:567
  69.6 0.0 copy-done.4
  69.6 0.7 copy.21
  70.3 0.0 copy-done
  70.3 0.0 copy-start.1
  70.3 1.1 %copy.22 = f32[800,200]{0,1:T(8,128)} copy(f32[800,200]{1,0:T(8,128)S(1)} %copy-done) | data formatting | bytes 1280000
  71.4 0.0 copy-done.1
  71.4 0.9 %copy.28 = f32[200,800]{1,0:T(8,128)} copy(f32[200,800]{1,0:T(8,128)S(1)} %copy-done.1) | data formatting | bytes 1280000
Async XLA Ops:
  2.0 1.6 %copy-start.5 = (f32[200]{0:T(256)S(1)}, f32[200]{0:T(256)}, u32[]{:S(2)}) copy-start(f32[200]{0:T(256)} %param.10) | copy-start | bytes 2404
  4.3 1.9 %copy-start.2 = (bf16[1,200,8,128]{3,2,1,0:T(8,128)(2,1)S(1)}, bf16[1,200,8,128]{3,2,1,0:T(8,128)(2,1)}, u32[]{:S(2)}) copy-start(bf16[1,200,8,128]{3,2,1,0:T(8,128)(2,1)} %param.7) | copy-start | bytes 1228804
  6.2 1.1 %copy-start.3 = (bf16[800,200]{0,1:T(8,128)(2,1)S(1)}, bf16[800,200]{0,1:T(8,128)(2,1)}, u32[]{:S(2)}) copy-start(bf16[800,200]{0,1:T(8,128)(2,1)} %param.12) | copy-start | bytes 960004
  66.0 4.2 %copy-start = (f32[800,200]{1,0:T(8,128)S(1)}, f32[800,200]{1,0:T(8,128)}, u32[]{:S(2)}) copy-start(f32[800,200]{1,0:T(8,128)} %get-tuple-element.24) | copy-start | bytes 1920004
  68.0 1.6 %copy-start.4 = (f32[200,49]{1,0:T(8,128)S(1)}, f32[200,49]{1,0:T(8,128)}, u32[]{:S(2)}) copy-start(f32[200,49]{1,0:T(8,128)} %get-tuple-element.21) | copy-start | bytes 117604
  70.3 1.1 %copy-start.1 = (f32[200,800]{1,0:T(8,128)S(1)}, f32[200,800]{1,0:T(8,128)}, u32[]{:S(2)}) copy-start(f32[200,800]{1,0:T(8,128)} %get-tuple-element.35) | copy-start | bytes 1920004

commit v4 on v3

--- a/solution.py
+++ b/solution.py
@@ -397,7 +397,7 @@
     dw_ref,
     gain_ref,
     expand_ref,
-    reduce_ref,
+    reduce_t,
     state_out,
     expand_out,
     reduce_out,
@@ -406,7 +406,9 @@
     main_ref,
     edge_ref,
     expand_t,
-    reduce_t,
+    reduce_ref,
+    table,
+    table_t,
     conv,
     scaled_all,
     hidden_all,
@@ -439,34 +441,46 @@
     for low, high in spans:
         piece = expand_ref[:, low:high].astype(jnp.float32).T
         expand_t[low:high, :] = piece.astype(jnp.bfloat16)
-        piece = reduce_ref[low:high, :].astype(jnp.float32).T
-        reduce_t[:, low:high] = piece.astype(jnp.bfloat16)
+        piece = reduce_t[:, low:high].astype(jnp.float32).T
+        reduce_ref[low:high, :] = piece.astype(jnp.bfloat16)
+    table[...] = jnp.zeros_like(table)
+    table[: KS * KS, :channels] = dw_ref[...]
+    table[KS * KS : KS * KS + 1, :channels] = gain_ref[...]
+    columns = table[...].T
+    table_t[...] = columns
+    gain = columns[:channels, KS * KS : KS * KS + 1]
     halo.spread_rows()
     halo.forward_corners()
-    halo.finish()
     lane = lax.broadcasted_iota(jnp.int32, (8, width), 1)
 
-    def conv_step(step, carry):
+    def conv_step(part, first, step, carry):
         rows = pl.ds(pl.multiple_of(step * 8, 8), 8)
-        taps = dw_ref[rows, :]
-        sums = [jnp.zeros((8, width), jnp.float32) for _ in range(tile_rows)]
+        taps = table_t[rows, :]
+        spans_of = [slice(row * width, (row + 1) * width) for row in range(tile_rows)]
+        if first:
+            sums = [jnp.zeros((8, width), jnp.float32) for _ in range(tile_rows)]
+        else:
+            sums = [conv[rows, one] for one in spans_of]
         for shift_b in range(KS):
             weights = [
                 jnp.broadcast_to(taps[:, a * KS + shift_b : a * KS + shift_b + 1], (8, width))
                 for a in range(KS)
             ]
-            for row in range(tile_rows + 2 * margin):
+            for row in part:
                 cells = window(main_ref[row, rows, :], edge_ref[row, rows, :], lane, shift_b - margin)
                 for shift_a in range(KS):
                     if 0 <= row - shift_a < tile_rows:
                         sums[row - shift_a] = sums[row - shift_a] + weights[shift_a] * cells
         for row in range(tile_rows):
-            conv[rows, row * width : (row + 1) * width] = sums[row]
+            conv[rows, spans_of[row]] = sums[row]
         return carry
 
-    lax.fori_loop(0, eights, conv_step, 0)
-
-    gain = gain_ref[...]
+    inner = range(margin, margin + tile_rows)
+    outer = [row for row in range(tile_rows + 2 * margin) if row not in inner]
+    lax.fori_loop(0, eights, functools.partial(conv_step, inner, True), 0)
+    halo.finish()
+    lax.fori_loop(0, eights, functools.partial(conv_step, outer, False), 0)
+
     block_rows = 2
     block = block_rows * width
 
@@ -506,15 +520,15 @@
     lax.fori_loop(0, tile_rows // block_rows, cell_step, 0)
 
     over_cells = (((1,), (1,)), ((), ()))
-    for at, (low, high) in enumerate(spans):
-        grad = lax.dot_general(
-            scaled_all[...], d_pre_all[low:high, :], over_cells, preferred_element_type=jnp.float32
-        )
-        pack(big.acc, at * 2 * eights, 0, grad * scale)
-        grad = lax.dot_general(
-            cot_ref[...], hidden_all[low:high, :], over_cells, preferred_element_type=jnp.float32
-        )
-        pack(big.acc, at * 2 * eights, eights, grad * scale)
+    for low in range(0, hidden_units, 2 * LANES):
+        high = min(low + 2 * LANES, hidden_units)
+        for turn, (left, right) in enumerate([(scaled_all, d_pre_all), (cot_ref, hidden_all)]):
+            grad = lax.dot_general(
+                left[...], right[low:high, :], over_cells, preferred_element_type=jnp.float32
+            )
+            for first, last in lane_spans(high - low):
+                at = (low + first) // LANES
+                pack(big.acc, at * 2 * eights, turn * eights, grad[:, first:last] * scale)
 
     def depthwise_step(step, carry):
         rows = pl.ds(pl.multiple_of(step * 8, 8), 8)
@@ -547,10 +561,13 @@
         both = big.full[at * eights : (at + 1) * eights].astype(jnp.float32)
         both = both.reshape(2 * channels, LANES)
         expand_out[:, low:high] = both[:channels, : high - low]
-        reduce_out[low:high, :] = both[channels:].T[: high - low, :]
-    rest = small.full[: -(-eights // 2)].astype(jnp.float32).reshape(-1, LANES)
-    taps_out[...] = rest[:channels, : KS * KS]
-    gain_out[...] = rest[:channels, KS * KS : KS * KS + 1]
+        reduce_out[:, low:high] = both[channels:, : high - low]
+    table_t[:channels] = (
+        small.full[: -(-eights // 2)].astype(jnp.float32).reshape(-1, LANES)[:channels]
+    )
+    lines = table_t[...].T
+    taps_out[...] = lines[: KS * KS, :channels]
+    gain_out[...] = lines[KS * KS : KS * KS + 1, :channels]
     halo.drain()
 
 
@@ -569,9 +586,9 @@
         out_shape=(
             jax.ShapeDtypeStruct((channels, cells), jnp.bfloat16),
             jax.ShapeDtypeStruct((channels, hidden), jnp.float32),
-            jax.ShapeDtypeStruct((hidden, channels), jnp.float32),
-            jax.ShapeDtypeStruct((channels, KS * KS), jnp.float32),
-            jax.ShapeDtypeStruct((channels, 1), jnp.float32),
+            jax.ShapeDtypeStruct((channels, hidden), jnp.float32),
+            jax.ShapeDtypeStruct((KS * KS, channels), jnp.float32),
+            jax.ShapeDtypeStruct((1, channels), jnp.float32),
         ),
         in_specs=[vmem] * 7,
         out_specs=[vmem] * 5,
@@ -579,7 +596,9 @@
             padded,
             padded,
             pltpu.VMEM((hidden, channels), jnp.bfloat16),
-            pltpu.VMEM((channels, hidden), jnp.bfloat16),
+            pltpu.VMEM((hidden, channels), jnp.bfloat16),
+            pltpu.VMEM((LANES, -(-channels // LANES) * LANES), jnp.float32),
+            pltpu.VMEM((-(-channels // LANES) * LANES, LANES), jnp.float32),
             pltpu.VMEM((channels, cells), jnp.float32),
             pltpu.VMEM((channels, cells), jnp.bfloat16),
             pltpu.VMEM((hidden, cells), jnp.bfloat16),
@@ -592,7 +611,7 @@
         compiler_params=pltpu.CompilerParams(
             collective_id=0, has_side_effects=True, vmem_limit_bytes=60 * 1024 * 1024
         ),
-    )(masked, cot, mask, dw_weight, norm_gain[:, None], expand_weight, reduce_weight)
+    )(masked, cot, mask, dw_weight.T, norm_gain[None, :], expand_weight, reduce_weight.T)
 
 
 def body(ocean_state, ocean_mask, dw_weight, norm_gain, expand_weight, reduce_weight, cotangent):
@@ -616,7 +635,7 @@
         reduce_weight,
     )
     next_state = out_flat.reshape(channels, tile_rows, tile_cols)[None]
-    return (next_state, taps, gain[:, 0], grad_expand, grad_reduce)
+    return (next_state, taps.T, gain[0], grad_expand, grad_reduce.T)
 
 
 def solution(mesh):

time: 72.6 us -> 70.4 us (0.970)
  other arithmetic: 5.63 us -> 3.27 us
  Pallas kernels: 57.8 us -> 60.1 us
  local copies, waits for them, and re-layouts: 8.15 us -> 6.06 us
    pallas_call x1, Pallas kernels: 57.8 us -> 60.1 us  [block_call(): pl.pallas_call(functools.partial(block_kernel, big, small, halo, scale),...]
    pallas_call x1 -> x0, other arithmetic: 1.6 us -> none  [block_call(): pl.pallas_call(functools.partial(block_kernel, big, small, halo, scale),...]
    unnamed x18 -> x17, local copies, waits for them, and re-layouts: 7.39 us -> 6.06 us
    convert_element_type x1, other arithmetic: 1.36 us -> 0.59 us  [body(): ocean_mask.astype(jnp.float32).reshape(1, cell_count)]
    broadcast_in_dim x1 -> x0, local copies, waits for them, and re-layouts: 0.76 us -> none  [block_call(): norm_gain[:, None]]
where the time goes in v4:
time: 70.4 us; the launch traced here: 70.1 us
  Pallas kernels  60.1 us (85%)
  local copies, waits for them, and re-layouts  6.06 us (9%)
  other arithmetic  3.27 us (5%)
    pallas_call x1, Pallas kernels, block_call(): pl.pallas_call(functools.partial(block_kernel, big, small, halo, scale),...  60.1 us
    unnamed x17, local copies, waits for them, and re-layouts  6.06 us
    mul x1, other arithmetic, body(): cot_masked = (cotangent[0] * mask_bf[None]).reshape(channels, cell_count)  1.86 us

profile of v4, /device:TPU:0, one launch (start us, length us, event | category | flops | bytes accessed | tf_op | source)
XLA Modules:
  0.0 70.1 jit_solution(5527606472535562007)
XLA Ops:
  0.6 0.0 copy-start.4
  0.6 0.7 copy-done.4
  1.3 0.6 fusion.1
  1.9 0.0 copy-start.2
  1.9 1.9 %bitcast_multiply_fusion.cot_ref = bf16[200,1024]{1,0:T(8,128)(2,1)} fusion(bf16[25,8,8,128]{3,2,1,0:T(8,128)(2,1)} %bitcast.22, bf16[1024]{0:T(1024)(128)(2,1)S(1)} %bitcast.28), kind=kLoop, calls=%fused_computation | loop fusion | flops 204800 | bytes 821248 | tf_op jit(solution)/shard_map/mul | solution.py:623
  3.8 0.0 copy-done.2
  3.8 0.8 %fusion.cells_ref = bf16[8,200,128]{2,1,0:T(8,128)(2,1)} fusion(bf16[1,200,8,128]{3,2,1,0:T(8,128)(2,1)S(1)} %copy-done.2, bf16[8,128]{1,0:T(8,128)(2,1)S(1)} %get-tuple-element.16), kind=kLoop, calls=%fused_computation.2 | loop fusion | flops 204800 | bytes 821248 | tf_op jit(solution)/shard_map/transpose | solution.py:621
  4.6 60.1 %shard_map.110 = (bf16[200,1024]{1,0:T(8,128)(2,1)}, f32[200,800]{1,0:T(8,128)}, f32[200,800]{1,0:T(8,128)}, f32[49,200]{1,0:T(8,128)}, f32[1,200]{1,0:T(1,128)}) custom-call(bf16[8,200,128]{2,1,0:T(8,128)(2,1)} %fusion.cells_ref, bf16[200,1024]{1,0:T(8,128)(2,1)} %bitcast_multiply_fusion.cot_ref, f32[1,1024]{1,0:T(1,128)} %bitcast.29, f32[49,200]{1,0:T(8,128)} %bitcast.27, ...), custom_call_target="tpu_custom_call" | custom-call | tf_op jit(solution)/shard_map/pallas_call | solution.py:584
  64.7 0.0 copy-start.1
  64.7 0.0 copy-start.3
  64.7 1.9 %copy.14 = bf16[25,8,8,128]{3,2,1,0:T(8,128)(2,1)} copy(bf16[25,8,8,128]{3,1,2,0:T(8,128)(2,1)} %bitcast.24) | data formatting | bytes 819200
  66.6 0.0 copy-done.3
  66.6 0.0 copy-start.5
  66.6 0.6 copy.21
  67.2 0.0 copy-done.5
  67.3 0.6 copy.22
  67.8 0.0 copy-done.1
  67.8 0.0 copy-start
  67.9 0.9 %copy.23 = f32[200,800]{1,0:T(8,128)} copy(f32[200,800]{1,0:T(8,128)S(1)} %copy-done.1) | data formatting | bytes 1280000
  68.7 0.5 copy-done
  69.2 0.9 %copy.24 = f32[800,200]{0,1:T(8,128)} copy(f32[800,200]{0,1:T(8,128)S(1)} %bitcast.21) | data formatting | bytes 1280000
Async XLA Ops:
  0.6 0.7 copy-start.4
  1.9 1.9 %copy-start.2 = (bf16[1,200,8,128]{3,2,1,0:T(8,128)(2,1)S(1)}, bf16[1,200,8,128]{3,2,1,0:T(8,128)(2,1)}, u32[]{:S(2)}) copy-start(bf16[1,200,8,128]{3,2,1,0:T(8,128)(2,1)} %param.7) | copy-start | bytes 1228804
  64.7 3.2 %copy-start.1 = (f32[200,800]{1,0:T(8,128)S(1)}, f32[200,800]{1,0:T(8,128)}, u32[]{:S(2)}) copy-start(f32[200,800]{1,0:T(8,128)} %get-tuple-element.25) | copy-start | bytes 1920004
  64.7 1.9 %copy-start.3 = (f32[49,200]{1,0:T(8,128)S(1)}, f32[49,200]{1,0:T(8,128)}, u32[]{:S(2)}) copy-start(f32[49,200]{1,0:T(8,128)} %get-tuple-element.11) | copy-start | bytes 117604
  66.6 0.7 copy-start.5
  67.8 1.4 %copy-start = (f32[200,800]{1,0:T(8,128)S(1)}, f32[200,800]{1,0:T(8,128)}, u32[]{:S(2)}) copy-start(f32[200,800]{1,0:T(8,128)} %get-tuple-element.14) | copy-start | bytes 1920004

commit v5 on v4

--- a/solution.py
+++ b/solution.py
@@ -475,11 +475,9 @@
             conv[rows, spans_of[row]] = sums[row]
         return carry
 
-    inner = range(margin, margin + tile_rows)
-    outer = [row for row in range(tile_rows + 2 * margin) if row not in inner]
-    lax.fori_loop(0, eights, functools.partial(conv_step, inner, True), 0)
     halo.finish()
-    lax.fori_loop(0, eights, functools.partial(conv_step, outer, False), 0)
+    every = range(tile_rows + 2 * margin)
+    lax.fori_loop(0, eights, functools.partial(conv_step, every, True), 0)
 
     block_rows = 2
     block = block_rows * width

time: 70.4 us -> 67.6 us (0.960)
  Pallas kernels: 60.1 us -> 57.3 us
    pallas_call x1, Pallas kernels: 60.1 us -> 57.3 us  [block_call(): pl.pallas_call(functools.partial(block_kernel, big, small, halo, scale),...]
where the time goes in v5:
time: 67.6 us; the launch traced here: 67.3 us
  Pallas kernels  57.3 us (85%)
  local copies, waits for them, and re-layouts  6.06 us (9%)
  other arithmetic  3.27 us (5%)
    pallas_call x1, Pallas kernels, block_call(): pl.pallas_call(functools.partial(block_kernel, big, small, halo, scale),...  57.3 us
    unnamed x17, local copies, waits for them, and re-layouts  6.06 us
    mul x1, other arithmetic, body(): cot_masked = (cotangent[0] * mask_bf[None]).reshape(channels, cell_count)  1.86 us

profile of v5, /device:TPU:0, one launch (start us, length us, event | category | flops | bytes accessed | tf_op | source)
XLA Modules:
  0.0 67.3 jit_solution(1118429150257491205)
XLA Ops:
  0.6 0.0 copy-start.4
  0.6 0.7 %copy-done.4 = s32[8,128]{1,0:T(8,128)S(1)} copy-done((s32[8,128]{1,0:T(8,128)S(1)}, s32[8,128]{1,0:T(8,128)}, u32[]{:S(2)}) %copy-start.4) | copy-done | bytes 4120
  1.3 0.6 fusion.1
  1.9 0.0 copy-start.2
  1.9 1.9 %bitcast_multiply_fusion.cot_ref = bf16[200,1024]{1,0:T(8,128)(2,1)} fusion(bf16[25,8,8,128]{3,2,1,0:T(8,128)(2,1)} %bitcast.22, bf16[1024]{0:T(1024)(128)(2,1)S(1)} %bitcast.28), kind=kLoop, calls=%fused_computation | loop fusion | flops 204800 | bytes 821248 | tf_op jit(solution)/shard_map/mul | solution.py:621
  3.8 0.0 copy-done.2
  3.8 0.8 %fusion.cells_ref = bf16[8,200,128]{2,1,0:T(8,128)(2,1)} fusion(bf16[1,200,8,128]{3,2,1,0:T(8,128)(2,1)S(1)} %copy-done.2, bf16[8,128]{1,0:T(8,128)(2,1)S(1)} %get-tuple-element.16), kind=kLoop, calls=%fused_computation.2 | loop fusion | flops 204800 | bytes 821248 | tf_op jit(solution)/shard_map/transpose | solution.py:619
  4.6 57.3 %shard_map.110 = (bf16[200,1024]{1,0:T(8,128)(2,1)}, f32[200,800]{1,0:T(8,128)}, f32[200,800]{1,0:T(8,128)}, f32[49,200]{1,0:T(8,128)}, f32[1,200]{1,0:T(1,128)}) custom-call(bf16[8,200,128]{2,1,0:T(8,128)(2,1)} %fusion.cells_ref, bf16[200,1024]{1,0:T(8,128)(2,1)} %bitcast_multiply_fusion.cot_ref, f32[1,1024]{1,0:T(1,128)} %bitcast.29, f32[49,200]{1,0:T(8,128)} %bitcast.27, ...), custom_call_target="tpu_custom_call" | custom-call | tf_op jit(solution)/shard_map/pallas_call | solution.py:582
  61.9 0.0 copy-start.1
  61.9 0.0 copy-start.3
  61.9 1.9 %copy.14 = bf16[25,8,8,128]{3,2,1,0:T(8,128)(2,1)} copy(bf16[25,8,8,128]{3,1,2,0:T(8,128)(2,1)} %bitcast.24) | data formatting | bytes 819200
  63.8 0.0 copy-done.3
  63.8 0.0 copy-start.5
  63.8 0.6 copy.21
  64.4 0.0 copy-done.5
  64.5 0.6 copy.22
  65.0 0.0 copy-done.1
  65.0 0.0 copy-start
  65.0 0.9 %copy.23 = f32[200,800]{1,0:T(8,128)} copy(f32[200,800]{1,0:T(8,128)S(1)} %copy-done.1) | data formatting | bytes 1280000
  65.9 0.5 copy-done
  66.4 0.9 %copy.24 = f32[800,200]{0,1:T(8,128)} copy(f32[800,200]{0,1:T(8,128)S(1)} %bitcast.21) | data formatting | bytes 1280000
Async XLA Ops:
  0.6 0.7 %copy-start.4 = (s32[8,128]{1,0:T(8,128)S(1)}, s32[8,128]{1,0:T(8,128)}, u32[]{:S(2)}) copy-start(s32[8,128]{1,0:T(8,128)} %param.8) | copy-start | bytes 12292
  1.9 1.9 %copy-start.2 = (bf16[1,200,8,128]{3,2,1,0:T(8,128)(2,1)S(1)}, bf16[1,200,8,128]{3,2,1,0:T(8,128)(2,1)}, u32[]{:S(2)}) copy-start(bf16[1,200,8,128]{3,2,1,0:T(8,128)(2,1)} %param.7) | copy-start | bytes 1228804
  61.9 3.2 %copy-start.1 = (f32[200,800]{1,0:T(8,128)S(1)}, f32[200,800]{1,0:T(8,128)}, u32[]{:S(2)}) copy-start(f32[200,800]{1,0:T(8,128)} %get-tuple-element.25) | copy-start | bytes 1920004
  61.9 1.9 %copy-start.3 = (f32[49,200]{1,0:T(8,128)S(1)}, f32[49,200]{1,0:T(8,128)}, u32[]{:S(2)}) copy-start(f32[49,200]{1,0:T(8,128)} %get-tuple-element.11) | copy-start | bytes 117604
  63.8 0.7 copy-start.5
  65.0 1.4 %copy-start = (f32[200,800]{1,0:T(8,128)S(1)}, f32[200,800]{1,0:T(8,128)}, u32[]{:S(2)}) copy-start(f32[200,800]{1,0:T(8,128)} %get-tuple-element.14) | copy-start | bytes 1920004
